TPU v7x, 256 devices: a whole 4x4x8 slice. The times are simulated.
256 devices in a mesh: grp: 4 (over z_lo), seq: 64 (over y, z_hi, x, core).
Axes of the slice: x: 4, y: 4, z: 8 (z_hi: 2, z_lo: 4; z = z_hi * 4 + z_lo), core: 2. Of those that a mesh axis runs over, the one named last changes fastest.
Arguments:
- tokens: bfloat16 [64, 1024, 1024], P('seq', 'grp'), may hold values from -6 to 6
- lengths: int32 [64, 3], P('seq'), may hold values from 1 to 768, 1024 in all within a row
- in_gain: float32 [1024], replicated, may hold values from 0.25 to 1.75
- out_gain: float32 [1024], replicated, may hold values from 0.25 to 1.75
- w_in: bfloat16 [1024, 2560], replicated, may hold values from -0.1875 to 0.1875
- w_out: bfloat16 [1024, 1024], replicated, may hold values from -0.1875 to 0.1875
- w_qgate: float32 [1024, 8], replicated, may hold values from -0.1875 to 0.1875
- w_xgate: float32 [1024, 8], replicated, may hold values from -0.1875 to 0.1875
- item_table: bfloat16 [32768, 1024], P('seq'), may hold values from -6 to 6
- neg_owner: int32 [64, 2048, 1], P('seq', 'grp'), may hold values from 0 to 63; in each aligned block of 512 rows (0 to 511, 512 to 1023, ..., all dimensions but the last counted through in order) at most 16 rows name the same one
- neg_slot: int32 [64, 2048], P('seq', 'grp'), may hold values from 0 to 511
- pos_owner: int32 [64, 1024, 1], P('seq', 'grp'), may hold values from 0 to 63; in each aligned block of 256 rows (0 to 255, 256 to 511, ..., all dimensions but the last counted through in order) at most 8 rows name the same one
- pos_slot: int32 [64, 1024], P('seq', 'grp'), may hold values from 0 to 511
Outputs:
- losses: float32 [64, 1024], P('seq', 'grp')
- query_grad: bfloat16 [64, 1024, 1024], P('seq', 'grp')
- table_grad: float32 [32768, 1024], P('seq')
Inputs may be any that keep to these rules, and one draw needn't show every extreme that they name: `neg_owner`: in the 512 rows of one device no owner is named more than 16 times, a bound that some block reaches. `pos_owner`: in the 256 rows of one device no owner is named more than 8 times, a bound that some block reaches. `lengths`: each row sums to 1024; its largest is exactly 768.
All inputs are finite; a program needn't handle non-finite values.
Results may differ from a plain program's by a relative error of at most 0.014.
Values may be sent and summed in bfloat16 or wider, within the bound.
No kernel may reach another device: no remote copies, remote signals or barrier semaphores. Data moves between devices by JAX's collectives and lax.ppermute only.
A program may use at most 128 MiB of HBM per device.

v0:
```python
import math

import jax
import jax.numpy as jnp
from jax import lax
from jax.experimental import pallas as pl
from jax.experimental.pallas import tpu as pltpu
from jax.sharding import Mesh
from jax.sharding import PartitionSpec as P

HEADS = 4
PARTS_SIZE = 8
INV_TEMP = 32.0
GATE_SCALE = 2.0

D = 1024
TOK = 256
NEG = 512
ITEMS = 512
CAPN = 16
CAPP = 8
CAP = CAPN + CAPP
PEERS = 32
HALF_ROWS = PEERS * CAP
QUARTER = ITEMS // 4
WIDTHS = (512, 512)
ATTEND_COST = 8 * 10**9
QKW = 256
PW = D // PARTS_SIZE
TILE = 16

PLANE = ("y", "x", "core")
SEQ = ("y", "zh", "x", "core")
COLUMN = ("zh", "grp")

F32 = jnp.float32
BF16 = jnp.bfloat16
HIGHEST = lax.Precision.HIGHEST


def matmul(a, b):
    return jnp.dot(a, b, preferred_element_type=F32)


def matmul_nt(a, b, precision=None):
    return lax.dot_general(a, b, (((1,), (1,)), ((), ())), precision=precision, preferred_element_type=F32)


def matmul_tn(a, b, precision=None):
    return lax.dot_general(a, b, (((0,), (0,)), ((), ())), precision=precision, preferred_element_type=F32)


def vmem_call(body, outs, n_smem=0, n_any=0, scratch=(), limit=50, flops=0, moved=0, name=None):
    def call(*args):
        in_specs = [pl.BlockSpec(memory_space=pltpu.SMEM)] * n_smem
        in_specs += [pl.BlockSpec(memory_space=pl.ANY)] * n_any
        in_specs += [pl.BlockSpec(memory_space=pltpu.VMEM)] * (len(args) - n_smem - n_any)
        return pl.pallas_call(
            body,
            out_shape=outs,
            in_specs=in_specs,
            out_specs=jax.tree.map(lambda _: pl.BlockSpec(memory_space=pltpu.VMEM), outs),
            scratch_shapes=list(scratch),
            compiler_params=pltpu.CompilerParams(vmem_limit_bytes=limit * 2**20),
            cost_estimate=pl.CostEstimate(flops=flops, bytes_accessed=moved, transcendentals=0),
            name=name,
        )(*args)

    return call


def pack_body(half_ref, nown_ref, nslot_ref, pown_ref, pslot_ref, ask_ref, place_ref, back_ref, owner_ref, slot_ref, sems):
    total = NEG + TOK
    pairs = (
        (nown_ref, owner_ref.at[:, :NEG]),
        (nslot_ref, slot_ref.at[:, :NEG]),
        (pown_ref, owner_ref.at[:, NEG:]),
        (pslot_ref, slot_ref.at[:, NEG:]),
    )
    copies = [pltpu.make_async_copy(a, b, sems.at[i]) for i, (a, b) in enumerate(pairs)]
    for copy in copies:
        copy.start()
    for copy in copies:
        copy.wait()
    owner = owner_ref[...]
    slot = slot_ref[...]
    lane = lax.broadcasted_iota(jnp.int32, (1, total), 1)
    positive = (lane >= NEG).astype(jnp.int32)
    far = ((owner >> 3) & 1) ^ half_ref[0]
    peer = (owner >> 4) * 8 + (owner & 7)
    key = positive * 64 + far * 32 + peer
    hot = key == lax.broadcasted_iota(jnp.int32, (128, total), 0)
    before = lax.broadcasted_iota(jnp.int32, (total, total), 0) < lax.broadcasted_iota(jnp.int32, (total, total), 1)
    counts = matmul(hot.astype(F32).astype(BF16), before.astype(F32).astype(BF16))
    rank = jnp.sum(jnp.where(hot, counts, 0.0), 0, keepdims=True).astype(jnp.int32)
    inner = rank + positive * CAPN
    column = far * CAP + inner
    peer_hot = (peer == lax.broadcasted_iota(jnp.int32, (PEERS, total), 0)).astype(F32).astype(BF16)
    here = column == lax.broadcasted_iota(jnp.int32, (2 * CAP, total), 0)
    value = slot + 1
    high = jnp.where(here, (value >> 5).astype(F32), 0.0).astype(BF16)
    low = jnp.where(here, (value & 31).astype(F32), 0.0).astype(BF16)
    ids = matmul_nt(peer_hot, high) * 32.0 + matmul_nt(peer_hot, low)
    ask_ref[...] = ids.astype(jnp.int32) - 1
    place_ref[...] = far * HALF_ROWS + peer * CAP + inner
    back_ref[...] = peer * (2 * CAP) + column


def pack(half, neg_owner, neg_slot, pos_owner, pos_slot):
    outs = (
        jax.ShapeDtypeStruct((PEERS, 2 * CAP), jnp.int32),
        jax.ShapeDtypeStruct((1, NEG + TOK), jnp.int32),
        jax.ShapeDtypeStruct((1, NEG + TOK), jnp.int32),
    )
    row = pltpu.VMEM((1, NEG + TOK), jnp.int32)
    return vmem_call(
        pack_body, outs, n_smem=1, n_any=4, scratch=[row, row, pltpu.SemaphoreType.DMA((4,))], name="pack"
    )(half, neg_owner, neg_slot, pos_owner, pos_slot)


def look_body(ids_ref, table_ref, rows_ref):
    hot = ids_ref[...] == lax.broadcasted_iota(jnp.int32, (HALF_ROWS, ITEMS), 1)
    rows_ref[...] = matmul(hot.astype(F32).astype(BF16), table_ref[...]).astype(BF16)


def look(ids, table, cost=1):
    outs = jax.ShapeDtypeStruct((HALF_ROWS, D), BF16)
    return vmem_call(look_body, outs, flops=cost * 2 * HALF_ROWS * ITEMS * D, moved=4 * 2**20, name="look")(ids, table)


def relay(own):
    up = lax.ppermute(own, "grp", [(0, 1), (1, 2), (2, 3)])
    down = lax.ppermute(own, "grp", [(1, 0), (2, 1), (3, 2)])
    two = lax.ppermute(own, "grp", [(i, (i + 2) % 4) for i in range(4)])
    end = lax.ppermute(two, "grp", [(2, 3), (1, 0)])
    return [own, up, down, two, end]


def lay_out(grp, refs, out_ref, cols):
    def put(at, ref):
        out_ref[pl.ds(pl.multiple_of(at * QUARTER, QUARTER), QUARTER), cols] = ref[...].astype(out_ref.dtype)

    own, up, down, two, end = refs
    put(grp, own)
    put((grp + 2) & 3, two)
    pl.when(grp > 0)(lambda: put(grp - 1, up))
    pl.when(grp < 3)(lambda: put(grp + 1, down))
    pl.when((grp == 0) | (grp == 3))(lambda: put(3 - grp, end))


def spread_body(grp_ref, *refs):
    out_ref = refs[-1]
    at = 0
    for i, width in enumerate(WIDTHS):
        lay_out(grp_ref[0], refs[5 * i : 5 * i + 5], out_ref, slice(at, at + width))
        at += width


def spread(grp, quarters):
    outs = jax.ShapeDtypeStruct((ITEMS, D), F32)
    return vmem_call(spread_body, outs, n_smem=1, moved=3 * 2**20, name="spread")(grp, *quarters)


def column_hop(value, step, senders):
    place = [(i % 4) * 2 + i // 4 for i in range(8)]
    pairs = [(place[i], place[(i + step) % 8]) for i in range(8) if i % 4 in senders]
    return lax.ppermute(value, ("grp", "zh"), pairs)


def add_body(ids_ref, grads_ref, *piece_refs):
    eighth = 2 * ITEMS // 8
    for pair in range(4):
        row = lax.broadcasted_iota(jnp.int32, (2 * eighth, 2 * HALF_ROWS), 0) + pair * 2 * eighth
        hot = (ids_ref[...] == row).astype(F32).astype(BF16)
        summed = matmul(hot, grads_ref[...]).astype(BF16)
        for i in range(2):
            at = 0
            for part, width in enumerate(WIDTHS):
                ref = piece_refs[8 * part + 2 * pair + i]
                ref[...] = summed[i * eighth : (i + 1) * eighth, at : at + width]
                at += width


def add_up(ids, grads):
    outs = sum(((jax.ShapeDtypeStruct((ITEMS // 4, width), BF16),) * 8 for width in WIDTHS), ())
    return vmem_call(add_body, outs, flops=8 * HALF_ROWS * ITEMS * D, moved=5 * 2**20, name="add_up")(ids, grads)


def ring_sum(pieces):
    def hop(value, step):
        return column_hop(value, step, range(4))

    def plus(value, piece):
        return (value.astype(F32) + piece.astype(F32)).astype(BF16)

    back = hop(pieces[4], -1)
    ahead = hop(pieces[3], 1)
    back = hop(plus(back, pieces[5]), -1)
    ahead = hop(plus(ahead, pieces[2]), 1)
    back = hop(plus(back, pieces[6]), -1)
    ahead = hop(plus(ahead, pieces[1]), 1)
    back = hop(plus(back, pieces[7]), -1)
    return (pieces[0].astype(F32) + back.astype(F32) + ahead.astype(F32)).astype(BF16)


def layer_norm(values, gain_vec):
    average = jnp.mean(values, -1, keepdims=True)
    centred = values - average
    spread = jnp.mean(centred * centred, -1, keepdims=True)
    return centred * lax.rsqrt(spread + 1e-05) * gain_vec


def front_body(tok_ref, gain_ref, w_ref, gq_ref, kv_ref):
    normed = layer_norm(tok_ref[...].astype(F32), gain_ref[...]).astype(BF16)

    def project(first, size):
        half = 0.5 * matmul(normed, w_ref[:, first : first + size])
        return (half + half * jnp.tanh(half)).astype(BF16)

    for at in range(0, D, 512):
        kv_ref[:, at : at + 512] = project(D + at, 512)
    kv_ref[:, D:] = project(2 * D + QKW, QKW)
    for at in range(0, D, 512):
        gq_ref[:, at : at + 512] = project(at, 512)
    gq_ref[:, D:] = project(2 * D, QKW)


def front_kernel(own_tokens, in_gain, w_in):
    out = jax.ShapeDtypeStruct((TOK, D + QKW), BF16)
    return vmem_call(front_body, (out, out), flops=14 * 10**8, moved=7 * 2**20, name="front")(own_tokens, in_gain, w_in)


def attend_blocks(grp_ref, len_ref, gq_ref, kv_refs, first):
    start = grp_ref[0] * TOK
    ends = [len_ref[0, 0]]
    for i in range(1, len_ref.shape[1]):
        ends.append(ends[-1] + len_ref[0, i])

    def segment(pos):
        return sum((pos >= end).astype(jnp.int32) for end in ends)

    query_pos = start + lax.broadcasted_iota(jnp.int32, (TOK, 1), 0)
    query_seg = segment(query_pos)
    masks = []
    for hop in range(first, first + len(kv_refs)):
        key_pos = start - hop * TOK + lax.broadcasted_iota(jnp.int32, (1, TOK), 1)
        seen = (query_seg == segment(key_pos)) & (key_pos >= 0) & (key_pos <= query_pos)
        masks.append(jnp.where(seen, 0.5 / math.sqrt(QKW // HEADS), 0.0))
    qkh = QKW // HEADS
    vh = D // HEADS
    for head in range(HEADS):
        query = gq_ref[:, D + head * qkh : D + (head + 1) * qkh]
        acc = jnp.zeros((TOK, vh), F32)
        for mask, ref in zip(masks, kv_refs):
            key = ref[:, D + head * qkh : D + (head + 1) * qkh]
            value = ref[:, head * vh : (head + 1) * vh]
            scores = matmul_nt(query, key) * mask
            weights = (scores + scores * jnp.tanh(scores)).astype(BF16)
            acc = acc + matmul(weights, value)
        yield slice(head * vh, (head + 1) * vh), acc


def near_body(grp_ref, len_ref, gq_ref, kv0_ref, kv1_ref, kv2_ref, mixed_ref):
    for cols, acc in attend_blocks(grp_ref, len_ref, gq_ref, (kv0_ref, kv1_ref, kv2_ref), 0):
        mixed_ref[:, cols] = acc


def last_body(grp_ref, len_ref, tok_ref, gq_ref, part_ref, kv3_ref, gain_ref, wout_ref, out_ref, mixed_ref):
    for cols, acc in attend_blocks(grp_ref, len_ref, gq_ref, (kv3_ref,), 3):
        mixed_ref[:, cols] = part_ref[:, cols] + acc
    gated = (layer_norm(mixed_ref[...], gain_ref[...]) * gq_ref[:, :D].astype(F32)).astype(BF16)
    out_ref[...] = tok_ref[...].astype(F32) + matmul(gated, wout_ref[...])


def attend(grp, lengths, own_tokens, gq, kvs, out_gain, w_out):
    outs = jax.ShapeDtypeStruct((TOK, D), F32)
    part = vmem_call(near_body, outs, n_smem=2, flops=10**9, moved=4 * 2**20, name="attend_near")(
        grp, lengths, gq, *kvs[:3]
    )
    return vmem_call(
        last_body, outs, n_smem=2, scratch=[pltpu.VMEM((TOK, D), F32)], flops=ATTEND_COST, moved=8 * 2**20, name="attend_last"
    )(grp, lengths, own_tokens, gq, part, kvs[3], out_gain, w_out)


def gate_of(u):
    t = jnp.tanh(u)
    return t, jnp.exp(GATE_SCALE * t)


def split(values):
    high = values.astype(BF16).astype(F32)
    return high, values - high


def split_rows(values):
    high, rest = split(values)
    middle, low = split(rest)
    return jnp.concatenate([high, middle, low], 0).astype(BF16)


def loss_body(
    query_ref, near_ref, far_ref, place_ref, back_ref, wqt_ref, wxt_ref,
    loss_ref, qgrad_ref, grads_ref,
    x_ref, unit_ref, cos_ref, dcos_ref, dcosr_ref, side_ref, dqgate_ref, dxgate_ref, dx_ref, du_ref,
):
    lanes = lax.broadcasted_iota(jnp.int32, (NEG + TOK, HALF_ROWS), 1)
    hot_near = (place_ref[...] == lanes).astype(F32).astype(BF16)
    hot_far = (place_ref[...] == lanes + HALF_ROWS).astype(F32).astype(BF16)
    x_ref[...] = (matmul(hot_near, near_ref[...]) + matmul(hot_far, far_ref[...])).astype(BF16)

    part_of = lax.broadcasted_iota(jnp.int32, (16, D), 1) // PW
    pick = (part_of == lax.broadcasted_iota(jnp.int32, (16, D), 0)).astype(F32).astype(BF16)
    eye = lax.broadcasted_iota(jnp.int32, (1, PARTS_SIZE), 1)

    rows = x_ref[...].astype(F32)
    high, low = split(rows * rows)
    squares = matmul_nt(high.astype(BF16), pick) + matmul_nt(low.astype(BF16), pick)
    x_norms = lax.rsqrt(squares[:, :PARTS_SIZE] + 1e-06)
    terms = matmul_nt(x_ref[...], split_rows(wxt_ref[...]))
    xgate = terms[:, :8] + terms[:, 8:16] + terms[:, 16:]
    side = jnp.concatenate([xgate[:NEG], x_norms[:NEG], jnp.zeros((NEG, 112), F32)], 1)
    side_ref[...] = jnp.transpose(side)[:16, :]
    pgate = xgate[NEG:]

    query = query_ref[...]
    qgate = matmul_nt(query, wqt_ref[...], HIGHEST)

    pos_cos = jnp.zeros((TOK, PARTS_SIZE), F32)
    q_norms = []
    for p in range(PARTS_SIZE):
        cols = slice(p * PW, (p + 1) * PW)
        q_p = query_ref[:, cols]
        q_norm = lax.rsqrt(jnp.sum(q_p * q_p, -1, keepdims=True) + 1e-06)
        q_unit = q_p * q_norm
        unit_ref[:, cols] = q_unit
        q_high, q_low = split(q_unit)
        x_p = x_ref[:NEG, cols]
        q_two = jnp.concatenate([q_high.astype(BF16), q_low.astype(BF16)], 1)
        cos_ref[p] = matmul_nt(q_two, jnp.concatenate([x_p, x_p], 1)) * side_ref[8 + p : 9 + p, :]
        dot_p = jnp.sum(q_unit * x_ref[NEG:, cols].astype(F32), -1, keepdims=True)
        pos_cos = jnp.where(eye == p, dot_p, pos_cos)
        q_norms.append(q_norm)
    pos_cos = pos_cos * x_norms[NEG:]

    t_pos, e_pos = gate_of(qgate + pgate)
    mix_pos = e_pos / jnp.sum(e_pos, -1, keepdims=True)
    mean_pos = jnp.sum(mix_pos * pos_cos, -1, keepdims=True)
    pos_logit = INV_TEMP * mean_pos
    raised_pos = jnp.exp(pos_logit)

    dxgate_ref[...] = jnp.zeros_like(dxgate_ref)
    dqgate_ref[...] = qgate
    loss_ref[...] = raised_pos

    def tile(i, carry):
        rows = pl.ds(pl.multiple_of(i * TILE, TILE), TILE)
        qg = dqgate_ref[rows, :]
        qgs = [jnp.broadcast_to(qg[:, p : p + 1], (TILE, PW)) for p in range(PARTS_SIZE)]
        sums = [jnp.zeros((TILE, PW), F32) for _ in range(PARTS_SIZE)]
        part = jnp.zeros((TILE, PW), F32)
        for block in range(NEG // PW):
            cols = slice(block * PW, (block + 1) * PW)
            ts, es, cs = [], [], []
            total = jnp.zeros((TILE, PW), F32)
            mixed = jnp.zeros((TILE, PW), F32)
            for p in range(PARTS_SIZE):
                t, e = gate_of(qgs[p] + side_ref[p : p + 1, cols])
                c = cos_ref[p, rows, cols]
                total = total + e
                mixed = mixed + e * c
                ts.append(t)
                es.append(e)
                cs.append(c)
            inverse = 1.0 / total
            mean = mixed * inverse
            raised = jnp.exp(INV_TEMP * mean)
            part = part + raised
            scaled = raised * inverse
            for p in range(PARTS_SIZE):
                dcos = scaled * es[p]
                du = dcos * (cs[p] - mean) * (1.0 - ts[p] * ts[p])
                dcos_ref[p, rows, cols] = dcos.astype(BF16)
                dcosr_ref[p, rows, cols] = (dcos * side_ref[8 + p : 9 + p, cols]).astype(BF16)
                du_ref[p, :, cols] = du
                sums[p] = sums[p] + du
        partition = loss_ref[rows, :] + jnp.sum(part, -1, keepdims=True)
        factor = (GATE_SCALE * INV_TEMP) / partition
        dq = jnp.zeros((TILE, PARTS_SIZE), F32)
        for p in range(PARTS_SIZE):
            du = du_ref[p] * factor
            dxgate_ref[p] += du[:8] + du[8:]
            dq = jnp.where(eye == p, jnp.sum(sums[p], -1, keepdims=True), dq)
        dqgate_ref[rows, :] = dq * factor
        loss_ref[rows, :] = partition
        return carry

    lax.fori_loop(0, TOK // TILE, tile, 0, unroll=2)

    partition = loss_ref[...]
    loss_ref[...] = jnp.log(partition) - pos_logit
    share = INV_TEMP / partition
    dpos = INV_TEMP * (raised_pos / partition - 1.0)
    dcos_pos = dpos * mix_pos
    du_pos = dcos_pos * (pos_cos - mean_pos) * (GATE_SCALE - GATE_SCALE * t_pos * t_pos)
    dxgate = jnp.transpose(jnp.concatenate([jnp.sum(dxgate_ref[...], 1), jnp.zeros((120, NEG), F32)], 0))

    def by_gate(values):
        high, low = split(values)
        return jnp.concatenate([high, low, high], 1).astype(BF16)

    def gate_weights(values):
        high, low = split(values)
        return jnp.concatenate([high, high, low], 0).astype(BF16)

    dqgate = by_gate(dqgate_ref[...] + du_pos)
    dxgate = by_gate(jnp.concatenate([dxgate[:, :PARTS_SIZE], du_pos], 0))
    wq = gate_weights(wqt_ref[...])
    wx = gate_weights(wxt_ref[...])

    for p in range(PARTS_SIZE):
        cols = slice(p * PW, (p + 1) * PW)
        q_unit = unit_ref[:, cols]
        dc = dcos_pos[:, p : p + 1]
        p_norm = x_norms[NEG:, p : p + 1]
        p_unit = x_ref[NEG:, cols].astype(F32) * p_norm
        d_unit = matmul(dcosr_ref[p], x_ref[:NEG, cols]) * share + dc * p_unit
        along = jnp.sum(d_unit * q_unit, -1, keepdims=True)
        qgrad_ref[:, cols] = (q_norms[p] * (d_unit - q_unit * along) + matmul(dqgate, wq[:, cols])).astype(BF16)

        gate_term = matmul(dxgate, wx[:, cols])
        dpos_p = p_norm * dc * (q_unit - p_unit * pos_cos[:, p : p + 1]) + gate_term[NEG:]
        dx_ref[NEG:, cols] = dpos_p.astype(BF16)

        x_norm = x_norms[:NEG, p : p + 1]
        x_unit = x_ref[:NEG, cols].astype(F32) * x_norm
        d_unit = matmul_tn(dcos_ref[p], (q_unit * share).astype(BF16))
        along = jnp.sum(d_unit * x_unit, -1, keepdims=True)
        dx_ref[:NEG, cols] = (x_norm * (d_unit - x_unit * along) + gate_term[:NEG]).astype(BF16)

    for part in range(4):
        size = 2 * HALF_ROWS // 4
        row = lax.broadcasted_iota(jnp.int32, (size, NEG + TOK), 0) + part * size
        hot = (back_ref[...] == row).astype(F32).astype(BF16)
        grads_ref[part * size : (part + 1) * size, :] = matmul(hot, dx_ref[...]).astype(BF16)


def loss_and_grads(query, near, far, place, back, w_qgate, w_xgate):
    outs = (
        jax.ShapeDtypeStruct((TOK, 1), F32),
        jax.ShapeDtypeStruct((TOK, D), BF16),
        jax.ShapeDtypeStruct((2 * HALF_ROWS, D), BF16),
    )
    scratch = [
        pltpu.VMEM((NEG + TOK, D), BF16),
        pltpu.VMEM((TOK, D), F32),
        pltpu.VMEM((PARTS_SIZE, TOK, NEG), F32),
        pltpu.VMEM((PARTS_SIZE, TOK, NEG), BF16),
        pltpu.VMEM((PARTS_SIZE, TOK, NEG), BF16),
        pltpu.VMEM((2 * PARTS_SIZE, NEG), F32),
        pltpu.VMEM((TOK, PARTS_SIZE), F32),
        pltpu.VMEM((PARTS_SIZE, 8, NEG), F32),
        pltpu.VMEM((NEG + TOK, D), BF16),
        pltpu.VMEM((PARTS_SIZE, TILE, NEG), F32),
    ]
    return vmem_call(loss_body, outs, scratch=scratch, flops=8 * 10**9, moved=10 * 2**20, name="loss")(
        query, near, far, place.reshape(-1, 1), back, w_qgate.T, w_xgate.T
    )


def local(
    tokens,
    lengths,
    in_gain,
    out_gain,
    w_in,
    w_out,
    w_qgate,
    w_xgate,
    item_table,
    neg_owner,
    neg_slot,
    pos_owner,
    pos_slot,
):
    own_tokens = tokens[0]
    half = lax.axis_index("zh").astype(jnp.int32)[None]
    grp = lax.axis_index("grp").astype(jnp.int32)[None]
    barrier = lax.optimization_barrier

    quarter = lax.dynamic_slice_in_dim(item_table, grp[0] * QUARTER, QUARTER, 0)
    tables = lax.all_gather(quarter, COLUMN, tiled=True)

    gate_query, key_value = front_kernel(own_tokens, in_gain[None], w_in)
    kvs = [key_value]
    for _ in range(2):
        kvs.append(lax.ppermute(kvs[-1], "grp", [(i, i + 1) for i in range(3)]))

    half_then, _ = barrier((half, key_value))
    ask, place, back = pack(
        half_then,
        neg_owner.reshape(1, NEG),
        neg_slot.reshape(1, NEG),
        pos_owner.reshape(1, TOK),
        pos_slot.reshape(1, TOK),
    )
    asked = lax.all_to_all(ask, PLANE, split_axis=0, concat_axis=0, tiled=True)

    asked_then, _ = barrier((asked, key_value))
    near_ids = asked_then[:, :CAP].reshape(-1, 1)
    far_ids = asked_then[:, CAP:].reshape(-1, 1)
    looked = look(near_ids, item_table)
    near = lax.all_to_all(looked, PLANE, split_axis=0, concat_axis=0, tiled=True)

    far_ids, _ = barrier((far_ids, kvs[1]))
    far_table = lax.dynamic_slice_in_dim(tables, (1 - half[0]) * ITEMS, ITEMS, 0)
    looked = look(far_ids, far_table, 20)
    far = lax.all_to_all(looked, PLANE, split_axis=0, concat_axis=0, tiled=True)

    kvs[2], _ = barrier((kvs[2], looked))
    kvs.append(lax.ppermute(kvs[2], "grp", [(i, i + 1) for i in range(3)]))
    query = attend(grp, lengths, own_tokens, gate_query, kvs, out_gain[None], w_out)

    losses, query_grad, grads = loss_and_grads(query, near, far, place, back, w_qgate, w_xgate)

    came = lax.all_to_all(grads, PLANE, split_axis=0, concat_axis=0, tiled=True)
    shard = half[0] ^ (lax.broadcasted_iota(jnp.int32, asked.shape, 1) // CAP)
    row = (asked + shard * ITEMS - (half[0] * 4 + grp[0]) * QUARTER) & (2 * ITEMS - 1)
    pieces = add_up(jnp.where(asked >= 0, row, -1).reshape(1, -1), came)
    sums = [ring_sum(pieces[8 * part : 8 * part + 8]) for part in range(len(WIDTHS))]
    return (losses.reshape(1, TOK), query_grad[None], spread(grp, sum((relay(part) for part in sums), [])))


def solution(mesh):
    fine = Mesh(mesh.devices.reshape(4, 4, 2, 4, 2), ("grp", "y", "zh", "x", "core"))
    in_specs = (
        P(SEQ, "grp", None),
        P(SEQ, None),
        P(),
        P(),
        P(),
        P(),
        P(),
        P(),
        P(SEQ, None),
        P(SEQ, "grp", None),
        P(SEQ, "grp"),
        P(SEQ, "grp", None),
        P(SEQ, "grp"),
    )
    out_specs = (P(SEQ, "grp"), P(SEQ, "grp", None), P(SEQ, None))
    return jax.shard_map(local, mesh=fine, in_specs=in_specs, out_specs=out_specs, check_vma=False)
```

profile of v0, /device:TPU:4, one launch (start us, length us, event | category | flops | bytes accessed | tf_op | source)
XLA Modules:
  0.0 228.6 jit_solution(8806231356933609836)
XLA Ops:
  7.2 1.7 constant_dynamic-slice_fusion.1
  10.7 4.5 %front.1 = (bf16[256,1280]{1,0:T(8,128)(2,1)S(1)}, bf16[256,1280]{1,0:T(8,128)(2,1)S(1)}) custom-call(bf16[256,1024]{1,0:T(8,128)(2,1)S(1)} %bitcast.23, f32[1,1024]{1,0:T(1,128)S(1)} %bitcast.25, bf16[1024,2560]{1,0:T(8,128)(2,1)} %w_ref.1), custom_call_target="tpu_custom_call" | custom-call | flops 1400000000 | bytes 7340032 | tf_op jit(solution)/shard_map/front/pallas_call | solution.py:58
  15.2 4.7 %collective-permute-start = (bf16[256,1280]{1,0:T(8,128)(2,1)S(1)}, bf16[256,1280]{1,0:T(8,128)(2,1)}, u32[]{:S(2)}, u32[]{:S(2)}) collective-permute-start(bf16[256,1280]{1,0:T(8,128)(2,1)S(1)} %get-tuple-element.32.kv0_ref), channel_id=1, source_target_pairs={{0,64},{64,128},{128,192},{1,65},{65,129},{129,193},{2,66},{66,130... | collective-permute-start | bytes 1966088 | tf_op jit(solution)/shard_map/ppermute | solution.py:496
  21.1 7.6 %all-to-all-start = ((s32[32,1,48]{2,1,0:T(1,128)}), s32[32,1,48]{2,1,0:T(1,128)S(1)}, u32[]{:S(2)}, u32[]{:S(2)}) async-start(s32[32,1,48]{2,1,0:T(1,128)} %bitcast.7), calls=%async_computation | async-start | bytes 32768 | tf_op jit(solution)/shard_map/all_to_all | solution.py:506
  28.7 5.1 %all-to-all-done = s32[32,1,48]{2,1,0:T(1,128)S(1)} async-done(((s32[32,1,48]{2,1,0:T(1,128)}), s32[32,1,48]{2,1,0:T(1,128)S(1)}, u32[]{:S(2)}, u32[]{:S(2)}) %all-to-all-start) | async-done | bytes 6176 | tf_op jit(solution)/shard_map/all_to_all | solution.py:506
  34.2 2.2 look.3
  36.4 6.0 %all-to-all-start.1 = ((bf16[32,24,1024]{2,1,0:T(8,128)(2,1)}), bf16[32,24,1024]{2,1,0:T(8,128)(2,1)S(1)}, u32[]{:S(2)}, u32[]{:S(2)}) async-start(bf16[32,24,1024]{2,1,0:T(8,128)(2,1)} %bitcast.10), calls=%async_computation.1 | async-start | bytes 3145728 | tf_op jit(solution)/shard_map/all_to_all | solution.py:512
  42.6 5.4 %collective-permute-start.1 = (bf16[256,1280]{1,0:T(8,128)(2,1)}, bf16[256,1280]{1,0:T(8,128)(2,1)}, u32[]{:S(2)}, u32[]{:S(2)}) collective-permute-start(bf16[256,1280]{1,0:T(8,128)(2,1)} %collective-permute-done.kv1_ref), channel_id=1, source_target_pairs={{0,64},{64,128},{128,192},{1,65},{65,129},{129,193},{2,66},{66,130... | collective-permute-start | bytes 1966088 | tf_op jit(solution)/shard_map/ppermute | solution.py:496
  48.0 14.6 %all-gather.2.cloned.1.call-done = bf16[1024,1024]{1,0:T(8,128)(2,1)} async-done(((bf16[128,1024]{1,0:T(8,128)(2,1)}), bf16[1024,1024]{1,0:T(8,128)(2,1)}) %all-gather.2.cloned.1.call-update) | async-done | bytes 2097168 | tf_op jit(solution)/shard_map/all_gather | solution.py:491
  63.9 2.2 look.2
  66.1 8.0 %all-to-all-start.2 = ((bf16[32,24,1024]{2,1,0:T(8,128)(2,1)}), bf16[32,24,1024]{2,1,0:T(8,128)(2,1)}, u32[]{:S(2)}, u32[]{:S(2)}) async-start(bf16[32,24,1024]{2,1,0:T(8,128)(2,1)} %bitcast.12), calls=%async_computation.2 | async-start | bytes 3145728 | tf_op jit(solution)/shard_map/all_to_all | solution.py:517
  74.1 5.6 %collective-permute-start.2 = (bf16[256,1280]{1,0:T(8,128)(2,1)}, bf16[256,1280]{1,0:T(8,128)(2,1)}, u32[]{:S(2)}, u32[]{:S(2)}) collective-permute-start(bf16[256,1280]{1,0:T(8,128)(2,1)} %collective-permute-done.1.kv2_ref), channel_id=1, source_target_pairs={{0,64},{64,128},{128,192},{1,65},{65,129},{129,193},{2,66},{66,130... | collective-permute-start | bytes 1966088 | tf_op jit(solution)/shard_map/ppermute | solution.py:520
  81.0 2.5 %attend_near.1.part_ref = f32[256,1024]{1,0:T(8,128)S(1)} custom-call(s32[1]{0:T(128)} %bitcast.grp_ref, s32[1,3]{1,0:T(1,128)S(1)} %copy-done.13, bf16[256,1280]{1,0:T(8,128)(2,1)S(1)} %get-tuple-element.31.gq_ref, bf16[256,1280]{1,0:T(8,128)(2,1)S(1)} %copy-done.9, bf16[256,1280]{1,0:T(8,128)(2,1)} %collective-permute-done.kv1_ref, ...), custom_call_target="tpu_custom_call" | custom-call | flops 1000000000 | bytes 4194304 | tf_op jit(solution)/shard_map/attend_near/pallas_call | solution.py:58
  83.4 10.0 %collective-permute-done.2.kv3_ref = bf16[256,1280]{1,0:T(8,128)(2,1)} collective-permute-done((bf16[256,1280]{1,0:T(8,128)(2,1)}, bf16[256,1280]{1,0:T(8,128)(2,1)}, u32[]{:S(2)}, u32[]{:S(2)}) %collective-permute-start.2) | collective-permute-done | bytes 655392 | tf_op jit(solution)/shard_map/ppermute | solution.py:520
  93.4 3.3 %attend_last.1.query_ref = f32[256,1024]{1,0:T(8,128)S(1)} custom-call(s32[1]{0:T(128)} %bitcast.grp_ref, s32[1,3]{1,0:T(1,128)S(1)} %copy-done.13, bf16[256,1024]{1,0:T(8,128)(2,1)S(1)} %bitcast.24, bf16[256,1280]{1,0:T(8,128)(2,1)S(1)} %get-tuple-element.31.gq_ref, f32[256,1024]{1,0:T(8,128)S(1)} %attend_near.1.part_ref, ...), custom_call_target="tpu_custom_call" | custom-call | flops 8000000000 | bytes 8388608 | tf_op jit(solution)/shard_map/attend_last/pallas_call | solution.py:58
  99.0 19.8 %loss.1 = (f32[256,1]{1,0:T(8,128)S(1)}, bf16[256,1024]{1,0:T(8,128)(2,1)}, bf16[1536,1024]{1,0:T(8,128)(2,1)}) custom-call(f32[256,1024]{1,0:T(8,128)S(1)} %copy-done.15, bf16[768,1024]{1,0:T(8,128)(2,1)S(1)} %bitcast.22, bf16[768,1024]{1,0:T(8,128)(2,1)} %bitcast.13.far_ref, s32[768,1]{1,0:T(8,128)S(1)} %copy.22.place_ref, ...), custom_call_target="tpu_custom_call" | custom-call | flops 8000000000 | bytes 10485760 | tf_op jit(solution)/shard_map/loss/pallas_call | solution.py:58
  118.8 7.4 %all-to-all-start.3 = ((bf16[32,48,1024]{2,1,0:T(8,128)(2,1)}), bf16[32,48,1024]{2,1,0:T(8,128)(2,1)}, u32[]{:S(2)}, u32[]{:S(2)}) async-start(bf16[32,48,1024]{2,1,0:T(8,128)(2,1)} %bitcast.32), calls=%async_computation.3 | async-start | bytes 6291456 | tf_op jit(solution)/shard_map/all_to_all | solution.py:525
  127.7 36.4 %all-to-all-done.3 = bf16[32,48,1024]{2,1,0:T(8,128)(2,1)} async-done(((bf16[32,48,1024]{2,1,0:T(8,128)(2,1)}), bf16[32,48,1024]{2,1,0:T(8,128)(2,1)}, u32[]{:S(2)}, u32[]{:S(2)}) %all-to-all-start.3) | async-done | bytes 3145760 | tf_op jit(solution)/shard_map/all_to_all | solution.py:525
  164.1 5.3 %add_up.1 = (bf16[128,512]{1,0:T(8,128)(2,1)S(1)}, bf16[128,512]{1,0:T(8,128)(2,1)S(1)}, bf16[128,512]{1,0:T(8,128)(2,1)S(1)}, bf16[128,512]{1,0:T(8,128)(2,1)S(...) custom-call(s32[1,1536]{1,0:T(1,128)S(1)} %compare_select_fusion.ids, ...), custom_call_target="tpu_custom_call" | custom-call | flops 3221225472 | bytes 5242880 | tf_op jit(solution)/shard_map/add_up/pallas_call | solution.py:58
  169.4 3.1 %collective-permute-start.3 = (bf16[128,512]{1,0:T(8,128)(2,1)S(1)}, bf16[128,512]{1,0:T(8,128)(2,1)S(1)}, u32[]{:S(2)}, u32[]{:S(2)}) collective-permute-start(bf16[128,512]{1,0:T(8,128)(2,1)S(1)} %get-tuple-element.44), channel_id=1, source_target_pairs={{0,200},{64,0},{128,64},{192,128},{8,192},{72,8},{136,72},{200,136... | collective-permute-start | bytes 393224 | tf_op jit(solution)/shard_map/ppermute | solution.py:167
  172.5 3.2 %collective-permute-start.14 = (bf16[128,512]{1,0:T(8,128)(2,1)S(1)}, bf16[128,512]{1,0:T(8,128)(2,1)S(1)}, u32[]{:S(2)}, u32[]{:S(2)}) collective-permute-start(bf16[128,512]{1,0:T(8,128)(2,1)S(1)} %get-tuple-element.52), channel_id=1, source_target_pairs={{0,200},{64,0},{128,64},{192,128},{8,192},{72,8},{136,72},{200,136... | collective-permute-start | bytes 393224 | tf_op jit(solution)/shard_map/ppermute | solution.py:167
  176.3 3.0 %collective-permute-start.4 = (bf16[128,512]{1,0:T(8,128)(2,1)S(1)}, bf16[128,512]{1,0:T(8,128)(2,1)S(1)}, u32[]{:S(2)}, u32[]{:S(2)}) collective-permute-start(bf16[128,512]{1,0:T(8,128)(2,1)S(1)} %add_convert_fusion.11), channel_id=1, source_target_pairs={{0,200},{64,0},{128,64},{192,128},{8,192},{72,8},{136,72},{200,136... | collective-permute-start | bytes 393224 | tf_op jit(solution)/shard_map/ppermute | solution.py:167
  179.5 3.3 %collective-permute-start.15 = (bf16[128,512]{1,0:T(8,128)(2,1)S(1)}, bf16[128,512]{1,0:T(8,128)(2,1)S(1)}, u32[]{:S(2)}, u32[]{:S(2)}) collective-permute-start(bf16[128,512]{1,0:T(8,128)(2,1)S(1)} %add_convert_fusion.5), channel_id=1, source_target_pairs={{0,200},{64,0},{128,64},{192,128},{8,192},{72,8},{136,72},{200,136... | collective-permute-start | bytes 393224 | tf_op jit(solution)/shard_map/ppermute | solution.py:167
  183.0 3.3 %collective-permute-start.5 = (bf16[128,512]{1,0:T(8,128)(2,1)S(1)}, bf16[128,512]{1,0:T(8,128)(2,1)S(1)}, u32[]{:S(2)}, u32[]{:S(2)}) collective-permute-start(bf16[128,512]{1,0:T(8,128)(2,1)S(1)} %add_convert_fusion.10), channel_id=1, source_target_pairs={{0,200},{64,0},{128,64},{192,128},{8,192},{72,8},{136,72},{200,136... | collective-permute-start | bytes 393224 | tf_op jit(solution)/shard_map/ppermute | solution.py:167
  186.5 3.6 %collective-permute-start.16 = (bf16[128,512]{1,0:T(8,128)(2,1)S(1)}, bf16[128,512]{1,0:T(8,128)(2,1)S(1)}, u32[]{:S(2)}, u32[]{:S(2)}) collective-permute-start(bf16[128,512]{1,0:T(8,128)(2,1)S(1)} %add_convert_fusion.4), channel_id=1, source_target_pairs={{0,200},{64,0},{128,64},{192,128},{8,192},{72,8},{136,72},{200,136... | collective-permute-start | bytes 393224 | tf_op jit(solution)/shard_map/ppermute | solution.py:167
  190.4 3.5 %collective-permute-start.6 = (bf16[128,512]{1,0:T(8,128)(2,1)S(1)}, bf16[128,512]{1,0:T(8,128)(2,1)S(1)}, u32[]{:S(2)}, u32[]{:S(2)}) collective-permute-start(bf16[128,512]{1,0:T(8,128)(2,1)S(1)} %add_convert_fusion.9), channel_id=1, source_target_pairs={{0,200},{64,0},{128,64},{192,128},{8,192},{72,8},{136,72},{200,136... | collective-permute-start | bytes 393224 | tf_op jit(solution)/shard_map/ppermute | solution.py:167
  194.0 3.0 %collective-permute-start.17 = (bf16[128,512]{1,0:T(8,128)(2,1)S(1)}, bf16[128,512]{1,0:T(8,128)(2,1)S(1)}, u32[]{:S(2)}, u32[]{:S(2)}) collective-permute-start(bf16[128,512]{1,0:T(8,128)(2,1)S(1)} %add_convert_fusion.3), channel_id=1, source_target_pairs={{0,200},{64,0},{128,64},{192,128},{8,192},{72,8},{136,72},{200,136... | collective-permute-start | bytes 393224 | tf_op jit(solution)/shard_map/ppermute | solution.py:167
  198.6 2.7 %collective-permute-done.17 = bf16[128,512]{1,0:T(8,128)(2,1)S(1)} collective-permute-done((bf16[128,512]{1,0:T(8,128)(2,1)S(1)}, bf16[128,512]{1,0:T(8,128)(2,1)S(1)}, u32[]{:S(2)}, u32[]{:S(2)}) %collective-permute-start.17) | collective-permute-done | bytes 131104 | tf_op jit(solution)/shard_map/ppermute | solution.py:167
  201.4 2.2 collective-permute-start.23
  203.5 2.6 %collective-permute-start.10 = (bf16[128,512]{1,0:T(8,128)(2,1)S(1)}, bf16[128,512]{1,0:T(8,128)(2,1)S(1)}, u32[]{:S(2)}, u32[]{:S(2)}) collective-permute-start(bf16[128,512]{1,0:T(8,128)(2,1)S(1)} %add_convert_fusion.6.refs_0_), channel_id=1, source_target_pairs={{0,64},{64,128},{128,192},{1,65},{65,129},{129,193},{2,66},{66,130... | collective-permute-start | bytes 393224 | tf_op jit(solution)/shard_map/ppermute | solution.py:132
  207.5 4.6 %collective-permute-start.21 = (bf16[128,512]{1,0:T(8,128)(2,1)S(1)}, bf16[128,512]{1,0:T(8,128)(2,1)S(1)}, u32[]{:S(2)}, u32[]{:S(2)}) collective-permute-start(bf16[128,512]{1,0:T(8,128)(2,1)S(1)} %add_convert_fusion.refs_5_), channel_id=1, source_target_pairs={{0,64},{64,128},{128,192},{1,65},{65,129},{129,193},{2,66},{66,130... | collective-permute-start | bytes 393224 | tf_op jit(solution)/shard_map/ppermute | solution.py:132
  215.6 3.3 %collective-permute-done.13.refs_4_ = bf16[128,512]{1,0:T(8,128)(2,1)S(1)} collective-permute-done((bf16[128,512]{1,0:T(8,128)(2,1)S(1)}, bf16[128,512]{1,0:T(8,128)(2,1)S(1)}, u32[]{:S(2)}, u32[]{:S(2)}) %collective-permute-start.13) | collective-permute-done | bytes 131104 | tf_op jit(solution)/shard_map/ppermute | solution.py:135
  (98 shorter events, 20.5 us)
Async XLA Ops:
  7.2 55.4 %all-gather.2.cloned.1.call-start = ((), (), s32[]{:S(2)}) async-start(), calls=%async_computation.4 | async-start | bytes 2359296 | tf_op jit(solution)/shard_map/all_gather | solution.py:491
  10.7 23.5 %copy-start = (bf16[512,1024]{1,0:T(8,128)(2,1)S(1)}, bf16[512,1024]{1,0:T(8,128)(2,1)}, u32[]{:S(2)}) copy-start(bf16[512,1024]{1,0:T(8,128)(2,1)} %table_ref.1) | copy-start | bytes 3145732
  15.2 27.3 %collective-permute-start = (bf16[256,1280]{1,0:T(8,128)(2,1)S(1)}, bf16[256,1280]{1,0:T(8,128)(2,1)}, u32[]{:S(2)}, u32[]{:S(2)}) collective-permute-start(bf16[256,1280]{1,0:T(8,128)(2,1)S(1)} %get-tuple-element.32.kv0_ref), channel_id=1, source_target_pairs={{0,64},{64,128},{128,192},{1,65},{65,129},{129,193},{2,66},{66,130... | collective-permute-start | bytes 1966088 | tf_op jit(solution)/shard_map/ppermute | solution.py:496
  21.1 12.8 %all-to-all-start = ((s32[32,1,48]{2,1,0:T(1,128)}), s32[32,1,48]{2,1,0:T(1,128)S(1)}, u32[]{:S(2)}, u32[]{:S(2)}) async-start(s32[32,1,48]{2,1,0:T(1,128)} %bitcast.7), calls=%async_computation | async-start | bytes 32768 | tf_op jit(solution)/shard_map/all_to_all | solution.py:506
  36.4 29.7 %all-to-all-start.1 = ((bf16[32,24,1024]{2,1,0:T(8,128)(2,1)}), bf16[32,24,1024]{2,1,0:T(8,128)(2,1)S(1)}, u32[]{:S(2)}, u32[]{:S(2)}) async-start(bf16[32,24,1024]{2,1,0:T(8,128)(2,1)} %bitcast.10), calls=%async_computation.1 | async-start | bytes 3145728 | tf_op jit(solution)/shard_map/all_to_all | solution.py:512
  42.6 31.5 %collective-permute-start.1 = (bf16[256,1280]{1,0:T(8,128)(2,1)}, bf16[256,1280]{1,0:T(8,128)(2,1)}, u32[]{:S(2)}, u32[]{:S(2)}) collective-permute-start(bf16[256,1280]{1,0:T(8,128)(2,1)} %collective-permute-done.kv1_ref), channel_id=1, source_target_pairs={{0,64},{64,128},{128,192},{1,65},{65,129},{129,193},{2,66},{66,130... | collective-permute-start | bytes 1966088 | tf_op jit(solution)/shard_map/ppermute | solution.py:496
  66.1 27.3 %copy-start.12 = (f32[1024]{0:T(1024)S(1)}, f32[1024]{0:T(1024)}, u32[]{:S(2)}) copy-start(f32[1024]{0:T(1024)} %param.16) | copy-start | bytes 12292
  66.1 31.6 %all-to-all-start.2 = ((bf16[32,24,1024]{2,1,0:T(8,128)(2,1)}), bf16[32,24,1024]{2,1,0:T(8,128)(2,1)}, u32[]{:S(2)}, u32[]{:S(2)}) async-start(bf16[32,24,1024]{2,1,0:T(8,128)(2,1)} %bitcast.12), calls=%async_computation.2 | async-start | bytes 3145728 | tf_op jit(solution)/shard_map/all_to_all | solution.py:517
  74.1 19.3 %collective-permute-start.2 = (bf16[256,1280]{1,0:T(8,128)(2,1)}, bf16[256,1280]{1,0:T(8,128)(2,1)}, u32[]{:S(2)}, u32[]{:S(2)}) collective-permute-start(bf16[256,1280]{1,0:T(8,128)(2,1)} %collective-permute-done.1.kv2_ref), channel_id=1, source_target_pairs={{0,64},{64,128},{128,192},{1,65},{65,129},{129,193},{2,66},{66,130... | collective-permute-start | bytes 1966088 | tf_op jit(solution)/shard_map/ppermute | solution.py:520
  118.8 45.3 %all-to-all-start.3 = ((bf16[32,48,1024]{2,1,0:T(8,128)(2,1)}), bf16[32,48,1024]{2,1,0:T(8,128)(2,1)}, u32[]{:S(2)}, u32[]{:S(2)}) async-start(bf16[32,48,1024]{2,1,0:T(8,128)(2,1)} %bitcast.32), calls=%async_computation.3 | async-start | bytes 6291456 | tf_op jit(solution)/shard_map/all_to_all | solution.py:525
  169.4 6.9 %collective-permute-start.3 = (bf16[128,512]{1,0:T(8,128)(2,1)S(1)}, bf16[128,512]{1,0:T(8,128)(2,1)S(1)}, u32[]{:S(2)}, u32[]{:S(2)}) collective-permute-start(bf16[128,512]{1,0:T(8,128)(2,1)S(1)} %get-tuple-element.44), channel_id=1, source_target_pairs={{0,200},{64,0},{128,64},{192,128},{8,192},{72,8},{136,72},{200,136... | collective-permute-start | bytes 393224 | tf_op jit(solution)/shard_map/ppermute | solution.py:167
  172.5 6.9 %collective-permute-start.7 = (bf16[128,512]{1,0:T(8,128)(2,1)S(1)}, bf16[128,512]{1,0:T(8,128)(2,1)S(1)}, u32[]{:S(2)}, u32[]{:S(2)}) collective-permute-start(bf16[128,512]{1,0:T(8,128)(2,1)S(1)} %get-tuple-element.48), channel_id=1, source_target_pairs={{0,64},{64,128},{128,192},{192,8},{8,72},{72,136},{136,200},{200,0... | collective-permute-start | bytes 393224 | tf_op jit(solution)/shard_map/ppermute | solution.py:167
  172.5 7.0 %collective-permute-start.14 = (bf16[128,512]{1,0:T(8,128)(2,1)S(1)}, bf16[128,512]{1,0:T(8,128)(2,1)S(1)}, u32[]{:S(2)}, u32[]{:S(2)}) collective-permute-start(bf16[128,512]{1,0:T(8,128)(2,1)S(1)} %get-tuple-element.52), channel_id=1, source_target_pairs={{0,200},{64,0},{128,64},{192,128},{8,192},{72,8},{136,72},{200,136... | collective-permute-start | bytes 393224 | tf_op jit(solution)/shard_map/ppermute | solution.py:167
  175.7 7.1 %collective-permute-start.18 = (bf16[128,512]{1,0:T(8,128)(2,1)S(1)}, bf16[128,512]{1,0:T(8,128)(2,1)S(1)}, u32[]{:S(2)}, u32[]{:S(2)}) collective-permute-start(bf16[128,512]{1,0:T(8,128)(2,1)S(1)} %get-tuple-element.56), channel_id=1, source_target_pairs={{0,64},{64,128},{128,192},{192,8},{8,72},{72,136},{136,200},{200,0... | collective-permute-start | bytes 393224 | tf_op jit(solution)/shard_map/ppermute | solution.py:167
  176.3 6.6 %collective-permute-start.4 = (bf16[128,512]{1,0:T(8,128)(2,1)S(1)}, bf16[128,512]{1,0:T(8,128)(2,1)S(1)}, u32[]{:S(2)}, u32[]{:S(2)}) collective-permute-start(bf16[128,512]{1,0:T(8,128)(2,1)S(1)} %add_convert_fusion.11), channel_id=1, source_target_pairs={{0,200},{64,0},{128,64},{192,128},{8,192},{72,8},{136,72},{200,136... | collective-permute-start | bytes 393224 | tf_op jit(solution)/shard_map/ppermute | solution.py:167
  179.4 6.9 %collective-permute-start.8 = (bf16[128,512]{1,0:T(8,128)(2,1)S(1)}, bf16[128,512]{1,0:T(8,128)(2,1)S(1)}, u32[]{:S(2)}, u32[]{:S(2)}) collective-permute-start(bf16[128,512]{1,0:T(8,128)(2,1)S(1)} %add_convert_fusion.8), channel_id=1, source_target_pairs={{0,64},{64,128},{128,192},{192,8},{8,72},{72,136},{136,200},{200,0... | collective-permute-start | bytes 393224 | tf_op jit(solution)/shard_map/ppermute | solution.py:167
  179.5 6.9 %collective-permute-start.15 = (bf16[128,512]{1,0:T(8,128)(2,1)S(1)}, bf16[128,512]{1,0:T(8,128)(2,1)S(1)}, u32[]{:S(2)}, u32[]{:S(2)}) collective-permute-start(bf16[128,512]{1,0:T(8,128)(2,1)S(1)} %add_convert_fusion.5), channel_id=1, source_target_pairs={{0,200},{64,0},{128,64},{192,128},{8,192},{72,8},{136,72},{200,136... | collective-permute-start | bytes 393224 | tf_op jit(solution)/shard_map/ppermute | solution.py:167
  182.9 7.4 %collective-permute-start.19 = (bf16[128,512]{1,0:T(8,128)(2,1)S(1)}, bf16[128,512]{1,0:T(8,128)(2,1)S(1)}, u32[]{:S(2)}, u32[]{:S(2)}) collective-permute-start(bf16[128,512]{1,0:T(8,128)(2,1)S(1)} %add_convert_fusion.2), channel_id=1, source_target_pairs={{0,64},{64,128},{128,192},{192,8},{8,72},{72,136},{136,200},{200,0... | collective-permute-start | bytes 393224 | tf_op jit(solution)/shard_map/ppermute | solution.py:167
  183.0 7.4 %collective-permute-start.5 = (bf16[128,512]{1,0:T(8,128)(2,1)S(1)}, bf16[128,512]{1,0:T(8,128)(2,1)S(1)}, u32[]{:S(2)}, u32[]{:S(2)}) collective-permute-start(bf16[128,512]{1,0:T(8,128)(2,1)S(1)} %add_convert_fusion.10), channel_id=1, source_target_pairs={{0,200},{64,0},{128,64},{192,128},{8,192},{72,8},{136,72},{200,136... | collective-permute-start | bytes 393224 | tf_op jit(solution)/shard_map/ppermute | solution.py:167
  186.3 10.7 %collective-permute-start.9 = (bf16[128,512]{1,0:T(8,128)(2,1)S(1)}, bf16[128,512]{1,0:T(8,128)(2,1)S(1)}, u32[]{:S(2)}, u32[]{:S(2)}) collective-permute-start(bf16[128,512]{1,0:T(8,128)(2,1)S(1)} %add_convert_fusion.7), channel_id=1, source_target_pairs={{0,64},{64,128},{128,192},{192,8},{8,72},{72,136},{136,200},{200,0... | collective-permute-start | bytes 393224 | tf_op jit(solution)/shard_map/ppermute | solution.py:167
  186.5 7.5 %collective-permute-start.16 = (bf16[128,512]{1,0:T(8,128)(2,1)S(1)}, bf16[128,512]{1,0:T(8,128)(2,1)S(1)}, u32[]{:S(2)}, u32[]{:S(2)}) collective-permute-start(bf16[128,512]{1,0:T(8,128)(2,1)S(1)} %add_convert_fusion.4), channel_id=1, source_target_pairs={{0,200},{64,0},{128,64},{192,128},{8,192},{72,8},{136,72},{200,136... | collective-permute-start | bytes 393224 | tf_op jit(solution)/shard_map/ppermute | solution.py:167
  190.3 8.3 %collective-permute-start.20 = (bf16[128,512]{1,0:T(8,128)(2,1)S(1)}, bf16[128,512]{1,0:T(8,128)(2,1)S(1)}, u32[]{:S(2)}, u32[]{:S(2)}) collective-permute-start(bf16[128,512]{1,0:T(8,128)(2,1)S(1)} %add_convert_fusion.1), channel_id=1, source_target_pairs={{0,64},{64,128},{128,192},{192,8},{8,72},{72,136},{136,200},{200,0... | collective-permute-start | bytes 393224 | tf_op jit(solution)/shard_map/ppermute | solution.py:167
  190.4 6.6 %collective-permute-start.6 = (bf16[128,512]{1,0:T(8,128)(2,1)S(1)}, bf16[128,512]{1,0:T(8,128)(2,1)S(1)}, u32[]{:S(2)}, u32[]{:S(2)}) collective-permute-start(bf16[128,512]{1,0:T(8,128)(2,1)S(1)} %add_convert_fusion.9), channel_id=1, source_target_pairs={{0,200},{64,0},{128,64},{192,128},{8,192},{72,8},{136,72},{200,136... | collective-permute-start | bytes 393224 | tf_op jit(solution)/shard_map/ppermute | solution.py:167
  194.0 7.3 %collective-permute-start.17 = (bf16[128,512]{1,0:T(8,128)(2,1)S(1)}, bf16[128,512]{1,0:T(8,128)(2,1)S(1)}, u32[]{:S(2)}, u32[]{:S(2)}) collective-permute-start(bf16[128,512]{1,0:T(8,128)(2,1)S(1)} %add_convert_fusion.3), channel_id=1, source_target_pairs={{0,200},{64,0},{128,64},{192,128},{8,192},{72,8},{136,72},{200,136... | collective-permute-start | bytes 393224 | tf_op jit(solution)/shard_map/ppermute | solution.py:167
  197.1 10.3 %collective-permute-start.12 = (bf16[128,512]{1,0:T(8,128)(2,1)S(1)}, bf16[128,512]{1,0:T(8,128)(2,1)S(1)}, u32[]{:S(2)}, u32[]{:S(2)}) collective-permute-start(bf16[128,512]{1,0:T(8,128)(2,1)S(1)} %add_convert_fusion.6.refs_0_), channel_id=1, source_target_pairs={{0,128},{64,192},{128,0},{192,64},{1,129},{65,193},{129,1},{193,65... | collective-permute-start | bytes 393224 | tf_op jit(solution)/shard_map/ppermute | solution.py:134
  197.3 14.8 %collective-permute-start.11 = (bf16[128,512]{1,0:T(8,128)(2,1)S(1)}, bf16[128,512]{1,0:T(8,128)(2,1)S(1)}, u32[]{:S(2)}, u32[]{:S(2)}) collective-permute-start(bf16[128,512]{1,0:T(8,128)(2,1)S(1)} %add_convert_fusion.6.refs_0_), channel_id=1, source_target_pairs={{64,0},{128,64},{192,128},{65,1},{129,65},{193,129},{66,2},{130,66... | collective-permute-start | bytes 393224 | tf_op jit(solution)/shard_map/ppermute | solution.py:133
  201.4 12.0 %collective-permute-start.23 = (bf16[128,512]{1,0:T(8,128)(2,1)S(1)}, bf16[128,512]{1,0:T(8,128)(2,1)S(1)}, u32[]{:S(2)}, u32[]{:S(2)}) collective-permute-start(bf16[128,512]{1,0:T(8,128)(2,1)S(1)} %add_convert_fusion.refs_5_), channel_id=1, source_target_pairs={{0,128},{64,192},{128,0},{192,64},{1,129},{65,193},{129,1},{193,65... | collective-permute-start | bytes 393224 | tf_op jit(solution)/shard_map/ppermute | solution.py:134
  203.5 11.8 %collective-permute-start.10 = (bf16[128,512]{1,0:T(8,128)(2,1)S(1)}, bf16[128,512]{1,0:T(8,128)(2,1)S(1)}, u32[]{:S(2)}, u32[]{:S(2)}) collective-permute-start(bf16[128,512]{1,0:T(8,128)(2,1)S(1)} %add_convert_fusion.6.refs_0_), channel_id=1, source_target_pairs={{0,64},{64,128},{128,192},{1,65},{65,129},{129,193},{2,66},{66,130... | collective-permute-start | bytes 393224 | tf_op jit(solution)/shard_map/ppermute | solution.py:132
  206.2 9.5 %collective-permute-start.22 = (bf16[128,512]{1,0:T(8,128)(2,1)S(1)}, bf16[128,512]{1,0:T(8,128)(2,1)S(1)}, u32[]{:S(2)}, u32[]{:S(2)}) collective-permute-start(bf16[128,512]{1,0:T(8,128)(2,1)S(1)} %add_convert_fusion.refs_5_), channel_id=1, source_target_pairs={{64,0},{128,64},{192,128},{65,1},{129,65},{193,129},{66,2},{130,66... | collective-permute-start | bytes 393224 | tf_op jit(solution)/shard_map/ppermute | solution.py:133
  207.5 8.1 %collective-permute-start.21 = (bf16[128,512]{1,0:T(8,128)(2,1)S(1)}, bf16[128,512]{1,0:T(8,128)(2,1)S(1)}, u32[]{:S(2)}, u32[]{:S(2)}) collective-permute-start(bf16[128,512]{1,0:T(8,128)(2,1)S(1)} %add_convert_fusion.refs_5_), channel_id=1, source_target_pairs={{0,64},{64,128},{128,192},{1,65},{65,129},{129,193},{2,66},{66,130... | collective-permute-start | bytes 393224 | tf_op jit(solution)/shard_map/ppermute | solution.py:132
  212.0 6.9 %collective-permute-start.13 = (bf16[128,512]{1,0:T(8,128)(2,1)S(1)}, bf16[128,512]{1,0:T(8,128)(2,1)S(1)}, u32[]{:S(2)}, u32[]{:S(2)}) collective-permute-start(bf16[128,512]{1,0:T(8,128)(2,1)S(1)} %collective-permute-done.12.refs_3_), channel_id=1, source_target_pairs={{128,192},{64,0},{129,193},{65,1},{130,194},{66,2},{131,195},{67,3... | collective-permute-start | bytes 393224 | tf_op jit(solution)/shard_map/ppermute | solution.py:135
  213.4 7.0 %collective-permute-start.24 = (bf16[128,512]{1,0:T(8,128)(2,1)S(1)}, bf16[128,512]{1,0:T(8,128)(2,1)S(1)}, u32[]{:S(2)}, u32[]{:S(2)}) collective-permute-start(bf16[128,512]{1,0:T(8,128)(2,1)S(1)} %collective-permute-done.23.refs_8_), channel_id=1, source_target_pairs={{128,192},{64,0},{129,193},{65,1},{130,194},{66,2},{131,195},{67,3... | collective-permute-start | bytes 393224 | tf_op jit(solution)/shard_map/ppermute | solution.py:135
  (14 other events, 104.9 us)
Sparse Core Ops, SparseCore 0:
  10.4 52.1 all-gather.1
where the time goes:
time: 232 us; the launch traced here: 229 us
  starting transfers between devices  85.7 us (37%)
  waiting for transfers between devices  74.7 us (32%)
  Pallas kernels  42.5 us (18%)
  between operations  14.5 us (6%)
  local copies, waits for them, and re-layouts  9.36 us (4%)
    pallas_call x9, Pallas kernels, call(): pl.pallas_call(body, out_shape=outs, in_specs=in_specs, out_specs=jax.tre...  42.5 us
    all_to_all x1, waiting for transfers between devices, local(): came = lax.all_to_all(grads, PLANE, split_axis=0, concat_axis=0, tiled=True)  36.4 us
    ppermute x14, starting transfers between devices, column_hop(): return lax.ppermute(value, ('grp', 'zh'), pairs)  26.4 us
    all_gather x1, waiting for transfers between devices, local(): tables = lax.all_gather(quarter, COLUMN, tiled=True)  14.6 us
    ppermute x2, starting transfers between devices, local(): kvs.append(lax.ppermute(kvs[-1], 'grp', [(i, i + 1) for i in range(3)]))  10.1 us
    ppermute x1, waiting for transfers between devices, local(): kvs.append(lax.ppermute(kvs[2], 'grp', [(i, i + 1) for i in range(3)]))  9.99 us
    all_to_all x1, starting transfers between devices, local(): far = lax.all_to_all(looked, PLANE, split_axis=0, concat_axis=0, tiled=True)  7.98 us
    all_to_all x1, starting transfers between devices, local(): asked = lax.all_to_all(ask, PLANE, split_axis=0, concat_axis=0, tiled=True)  7.6 us
  transfers between devices with their start and end apart: 30, of which 10 were waited for; matrix products, arithmetic and copies ran while one was open for 2% of the time, Pallas kernels for 7%

commit v1 on v0

--- a/solution.py
+++ b/solution.py
@@ -24,7 +24,7 @@
 HALF_ROWS = PEERS * CAP
 QUARTER = ITEMS // 4
 WIDTHS = (512, 512)
-ATTEND_COST = 8 * 10**9
+ATTEND_COST = 4 * 10**10
 QKW = 256
 PW = D // PARTS_SIZE
 TILE = 16

time: 232 us -> 240 us (1.034)
  waiting for transfers between devices: 74.7 us -> 80.7 us
    all_to_all x1, waiting for transfers between devices: 0.01 us -> 14.6 us  [local(): far = lax.all_to_all(looked, PLANE, split_axis=0, concat_axis=0, tiled=True)]
    ppermute x1, waiting for transfers between devices: 9.99 us -> 0.78 us  [local(): kvs.append(lax.ppermute(kvs[2], 'grp', [(i, i + 1) for i in range(3)]))]
    ppermute x2, starting transfers between devices: 2.29 us -> 7.43 us  [relay(): two = lax.ppermute(own, 'grp', [(i, (i + 2) % 4) for i in range(4)])]
    ppermute x2, waiting for transfers between devices: 0.04 us -> 2.85 us  [local(): kvs.append(lax.ppermute(kvs[-1], 'grp', [(i, i + 1) for i in range(3)]))]
    ppermute x14, starting transfers between devices: 26.4 us -> 24 us  [column_hop(): return lax.ppermute(value, ('grp', 'zh'), pairs)]
  transfers between devices with their start and end apart: 30 -> 30, of which waited for: 10 -> 13; matrix products, arithmetic and copies ran while one was open for 2% -> 2% of each run, Pallas kernels for 7% -> 7%
where the time goes in v1:
time: 240 us; the launch traced here: 237 us
  starting transfers between devices  86.6 us (36%)
  waiting for transfers between devices  80.7 us (34%)
  Pallas kernels  43 us (18%)
  between operations  14.5 us (6%)
  local copies, waits for them, and re-layouts  10.5 us (4%)
    pallas_call x9, Pallas kernels, call(): pl.pallas_call(body, out_shape=outs, in_specs=in_specs, out_specs=jax.tre...  43 us
    all_to_all x1, waiting for transfers between devices, local(): came = lax.all_to_all(grads, PLANE, split_axis=0, concat_axis=0, tiled=True)  36.4 us
    ppermute x14, starting transfers between devices, column_hop(): return lax.ppermute(value, ('grp', 'zh'), pairs)  24 us
    all_to_all x1, waiting for transfers between devices, local(): far = lax.all_to_all(looked, PLANE, split_axis=0, concat_axis=0, tiled=True)  14.6 us
    all_gather x1, waiting for transfers between devices, local(): tables = lax.all_gather(quarter, COLUMN, tiled=True)  13.7 us
    ppermute x2, starting transfers between devices, local(): kvs.append(lax.ppermute(kvs[-1], 'grp', [(i, i + 1) for i in range(3)]))  9.92 us
    all_to_all x1, starting transfers between devices, local(): came = lax.all_to_all(grads, PLANE, split_axis=0, concat_axis=0, tiled=True)  7.69 us
    all_to_all x1, starting transfers between devices, local(): far = lax.all_to_all(looked, PLANE, split_axis=0, concat_axis=0, tiled=True)  7.6 us
  transfers between devices with their start and end apart: 30, of which 13 were waited for; matrix products, arithmetic and copies ran while one was open for 2% of the time, Pallas kernels for 7%

profile of v1, /device:TPU:4, one launch (start us, length us, event | category | flops | bytes accessed | tf_op | source)
XLA Modules:
  0.0 237.1 jit_solution(16309034398608983282)
XLA Ops:
  7.2 1.7 constant_dynamic-slice_fusion.1
  10.7 4.8 %front.1 = (bf16[256,1280]{1,0:T(8,128)(2,1)S(1)}, bf16[256,1280]{1,0:T(8,128)(2,1)}) custom-call(bf16[256,1024]{1,0:T(8,128)(2,1)S(1)} %bitcast.23, f32[1,1024]{1,0:T(1,128)S(1)} %bitcast.25, bf16[1024,2560]{1,0:T(8,128)(2,1)} %w_ref.1), custom_call_target="tpu_custom_call" | custom-call | flops 1400000000 | bytes 7340032 | tf_op jit(solution)/shard_map/front/pallas_call | solution.py:58
  15.4 4.7 %collective-permute-start = (bf16[256,1280]{1,0:T(8,128)(2,1)}, bf16[256,1280]{1,0:T(8,128)(2,1)}, u32[]{:S(2)}, u32[]{:S(2)}) collective-permute-start(bf16[256,1280]{1,0:T(8,128)(2,1)} %get-tuple-element.32.kv0_ref), channel_id=1, source_target_pairs={{0,64},{64,128},{128,192},{1,65},{65,129},{129,193},{2,66},{66,130... | collective-permute-start | bytes 1966088 | tf_op jit(solution)/shard_map/ppermute | solution.py:496
  21.3 7.6 %all-to-all-start = ((s32[32,1,48]{2,1,0:T(1,128)}), s32[32,1,48]{2,1,0:T(1,128)S(1)}, u32[]{:S(2)}, u32[]{:S(2)}) async-start(s32[32,1,48]{2,1,0:T(1,128)} %bitcast.7), calls=%async_computation | async-start | bytes 32768 | tf_op jit(solution)/shard_map/all_to_all | solution.py:506
  28.9 5.1 %all-to-all-done = s32[32,1,48]{2,1,0:T(1,128)S(1)} async-done(((s32[32,1,48]{2,1,0:T(1,128)}), s32[32,1,48]{2,1,0:T(1,128)S(1)}, u32[]{:S(2)}, u32[]{:S(2)}) %all-to-all-start) | async-done | bytes 6176 | tf_op jit(solution)/shard_map/all_to_all | solution.py:506
  34.4 2.2 look.3
  36.6 6.0 %all-to-all-start.1 = ((bf16[32,24,1024]{2,1,0:T(8,128)(2,1)}), bf16[32,24,1024]{2,1,0:T(8,128)(2,1)S(1)}, u32[]{:S(2)}, u32[]{:S(2)}) async-start(bf16[32,24,1024]{2,1,0:T(8,128)(2,1)} %bitcast.10), calls=%async_computation.1 | async-start | bytes 3145728 | tf_op jit(solution)/shard_map/all_to_all | solution.py:512
  43.7 5.3 %collective-permute-start.1 = (bf16[256,1280]{1,0:T(8,128)(2,1)}, bf16[256,1280]{1,0:T(8,128)(2,1)}, u32[]{:S(2)}, u32[]{:S(2)}) collective-permute-start(bf16[256,1280]{1,0:T(8,128)(2,1)} %collective-permute-done.kv1_ref), channel_id=1, source_target_pairs={{0,64},{64,128},{128,192},{1,65},{65,129},{129,193},{2,66},{66,130... | collective-permute-start | bytes 1966088 | tf_op jit(solution)/shard_map/ppermute | solution.py:496
  48.9 13.7 %all-gather.2.cloned.1.call-done = bf16[1024,1024]{1,0:T(8,128)(2,1)} async-done(((bf16[128,1024]{1,0:T(8,128)(2,1)}), bf16[1024,1024]{1,0:T(8,128)(2,1)}) %all-gather.2.cloned.1.call-update) | async-done | bytes 2097168 | tf_op jit(solution)/shard_map/all_gather | solution.py:491
  64.0 2.2 look.2
  66.2 2.0 collective-permute-done.1.kv2_ref
  68.2 5.2 %collective-permute-start.2 = (bf16[256,1280]{1,0:T(8,128)(2,1)}, bf16[256,1280]{1,0:T(8,128)(2,1)}, u32[]{:S(2)}, u32[]{:S(2)}) collective-permute-start(bf16[256,1280]{1,0:T(8,128)(2,1)} %collective-permute-done.1.kv2_ref), channel_id=1, source_target_pairs={{0,64},{64,128},{128,192},{1,65},{65,129},{129,193},{2,66},{66,130... | collective-permute-start | bytes 1966088 | tf_op jit(solution)/shard_map/ppermute | solution.py:520
  73.6 2.7 %attend_near.1.part_ref = f32[256,1024]{1,0:T(8,128)S(1)} custom-call(s32[1]{0:T(128)} %bitcast.grp_ref, s32[1,3]{1,0:T(1,128)S(1)} %copy-done.11, bf16[256,1280]{1,0:T(8,128)(2,1)S(1)} %get-tuple-element.31.gq_ref, bf16[256,1280]{1,0:T(8,128)(2,1)} %get-tuple-element.32.kv0_ref, bf16[256,1280]{1,0:T(8,128)(2,1)} %collective-permute-done.kv1_ref, ...), custom_call_target="tpu_custom_call" | custom-call | flops 1000000000 | bytes 4194304 | tf_op jit(solution)/shard_map/attend_near/pallas_call | solution.py:58
  77.3 7.6 %all-to-all-start.2 = ((bf16[32,24,1024]{2,1,0:T(8,128)(2,1)}), bf16[32,24,1024]{2,1,0:T(8,128)(2,1)}, u32[]{:S(2)}, u32[]{:S(2)}) async-start(bf16[32,24,1024]{2,1,0:T(8,128)(2,1)} %bitcast.12), calls=%async_computation.2 | async-start | bytes 3145728 | tf_op jit(solution)/shard_map/all_to_all | solution.py:517
  86.9 3.3 %attend_last.1.query_ref = f32[256,1024]{1,0:T(8,128)S(1)} custom-call(s32[1]{0:T(128)} %bitcast.grp_ref, s32[1,3]{1,0:T(1,128)S(1)} %copy-done.11, bf16[256,1024]{1,0:T(8,128)(2,1)S(1)} %bitcast.24, bf16[256,1280]{1,0:T(8,128)(2,1)S(1)} %get-tuple-element.31.gq_ref, f32[256,1024]{1,0:T(8,128)S(1)} %copy-done.13, ...), custom_call_target="tpu_custom_call" | custom-call | flops 40000000000 | bytes 8388608 | tf_op jit(solution)/shard_map/attend_last/pallas_call | solution.py:58
  91.2 14.6 %all-to-all-done.2 = bf16[32,24,1024]{2,1,0:T(8,128)(2,1)} async-done(((bf16[32,24,1024]{2,1,0:T(8,128)(2,1)}), bf16[32,24,1024]{2,1,0:T(8,128)(2,1)}, u32[]{:S(2)}, u32[]{:S(2)}) %all-to-all-start.2) | async-done | bytes 1572896 | tf_op jit(solution)/shard_map/all_to_all | solution.py:517
  107.1 19.9 %loss.1 = (f32[256,1]{1,0:T(8,128)S(1)}, bf16[256,1024]{1,0:T(8,128)(2,1)}, bf16[1536,1024]{1,0:T(8,128)(2,1)}) custom-call(f32[256,1024]{1,0:T(8,128)S(1)} %copy-done.15, bf16[768,1024]{1,0:T(8,128)(2,1)S(1)} %bitcast.22, bf16[768,1024]{1,0:T(8,128)(2,1)} %bitcast.13.far_ref, s32[768,1]{1,0:T(8,128)S(1)} %copy.22.place_ref, ...), custom_call_target="tpu_custom_call" | custom-call | flops 8000000000 | bytes 10485760 | tf_op jit(solution)/shard_map/loss/pallas_call | solution.py:58
  127.0 7.7 %all-to-all-start.3 = ((bf16[32,48,1024]{2,1,0:T(8,128)(2,1)}), bf16[32,48,1024]{2,1,0:T(8,128)(2,1)}, u32[]{:S(2)}, u32[]{:S(2)}) async-start(bf16[32,48,1024]{2,1,0:T(8,128)(2,1)} %bitcast.32), calls=%async_computation.3 | async-start | bytes 6291456 | tf_op jit(solution)/shard_map/all_to_all | solution.py:525
  136.1 36.4 %all-to-all-done.3 = bf16[32,48,1024]{2,1,0:T(8,128)(2,1)} async-done(((bf16[32,48,1024]{2,1,0:T(8,128)(2,1)}), bf16[32,48,1024]{2,1,0:T(8,128)(2,1)}, u32[]{:S(2)}, u32[]{:S(2)}) %all-to-all-start.3) | async-done | bytes 3145760 | tf_op jit(solution)/shard_map/all_to_all | solution.py:525
  172.6 5.3 %add_up.1 = (bf16[128,512]{1,0:T(8,128)(2,1)S(1)}, bf16[128,512]{1,0:T(8,128)(2,1)S(1)}, bf16[128,512]{1,0:T(8,128)(2,1)S(1)}, bf16[128,512]{1,0:T(8,128)(2,1)S(...) custom-call(s32[1,1536]{1,0:T(1,128)S(1)} %compare_select_fusion.ids, ...), custom_call_target="tpu_custom_call" | custom-call | flops 3221225472 | bytes 5242880 | tf_op jit(solution)/shard_map/add_up/pallas_call | solution.py:58
  177.9 1.9 collective-permute-start.3
  180.0 3.0 %collective-permute-start.14 = (bf16[128,512]{1,0:T(8,128)(2,1)S(1)}, bf16[128,512]{1,0:T(8,128)(2,1)S(1)}, u32[]{:S(2)}, u32[]{:S(2)}) collective-permute-start(bf16[128,512]{1,0:T(8,128)(2,1)S(1)} %get-tuple-element.52), channel_id=1, source_target_pairs={{0,200},{64,0},{128,64},{192,128},{8,192},{72,8},{136,72},{200,136... | collective-permute-start | bytes 393224 | tf_op jit(solution)/shard_map/ppermute | solution.py:167
  184.4 2.3 collective-permute-start.4
  187.1 3.0 %collective-permute-start.15 = (bf16[128,512]{1,0:T(8,128)(2,1)S(1)}, bf16[128,512]{1,0:T(8,128)(2,1)S(1)}, u32[]{:S(2)}, u32[]{:S(2)}) collective-permute-start(bf16[128,512]{1,0:T(8,128)(2,1)S(1)} %add_convert_fusion.5), channel_id=1, source_target_pairs={{0,200},{64,0},{128,64},{192,128},{8,192},{72,8},{136,72},{200,136... | collective-permute-start | bytes 393224 | tf_op jit(solution)/shard_map/ppermute | solution.py:167
  190.5 3.0 %collective-permute-start.5 = (bf16[128,512]{1,0:T(8,128)(2,1)S(1)}, bf16[128,512]{1,0:T(8,128)(2,1)S(1)}, u32[]{:S(2)}, u32[]{:S(2)}) collective-permute-start(bf16[128,512]{1,0:T(8,128)(2,1)S(1)} %add_convert_fusion.10), channel_id=1, source_target_pairs={{0,200},{64,0},{128,64},{192,128},{8,192},{72,8},{136,72},{200,136... | collective-permute-start | bytes 393224 | tf_op jit(solution)/shard_map/ppermute | solution.py:167
  193.8 3.6 %collective-permute-start.16 = (bf16[128,512]{1,0:T(8,128)(2,1)S(1)}, bf16[128,512]{1,0:T(8,128)(2,1)S(1)}, u32[]{:S(2)}, u32[]{:S(2)}) collective-permute-start(bf16[128,512]{1,0:T(8,128)(2,1)S(1)} %add_convert_fusion.4), channel_id=1, source_target_pairs={{0,200},{64,0},{128,64},{192,128},{8,192},{72,8},{136,72},{200,136... | collective-permute-start | bytes 393224 | tf_op jit(solution)/shard_map/ppermute | solution.py:167
  197.7 3.5 %collective-permute-start.6 = (bf16[128,512]{1,0:T(8,128)(2,1)S(1)}, bf16[128,512]{1,0:T(8,128)(2,1)S(1)}, u32[]{:S(2)}, u32[]{:S(2)}) collective-permute-start(bf16[128,512]{1,0:T(8,128)(2,1)S(1)} %add_convert_fusion.9), channel_id=1, source_target_pairs={{0,200},{64,0},{128,64},{192,128},{8,192},{72,8},{136,72},{200,136... | collective-permute-start | bytes 393224 | tf_op jit(solution)/shard_map/ppermute | solution.py:167
  201.3 3.0 %collective-permute-start.17 = (bf16[128,512]{1,0:T(8,128)(2,1)S(1)}, bf16[128,512]{1,0:T(8,128)(2,1)S(1)}, u32[]{:S(2)}, u32[]{:S(2)}) collective-permute-start(bf16[128,512]{1,0:T(8,128)(2,1)S(1)} %add_convert_fusion.3), channel_id=1, source_target_pairs={{0,200},{64,0},{128,64},{192,128},{8,192},{72,8},{136,72},{200,136... | collective-permute-start | bytes 393224 | tf_op jit(solution)/shard_map/ppermute | solution.py:167
  204.4 2.3 collective-permute-start.12
  208.1 5.1 %collective-permute-start.23 = (bf16[128,512]{1,0:T(8,128)(2,1)S(1)}, bf16[128,512]{1,0:T(8,128)(2,1)S(1)}, u32[]{:S(2)}, u32[]{:S(2)}) collective-permute-start(bf16[128,512]{1,0:T(8,128)(2,1)S(1)} %add_convert_fusion.refs_5_), channel_id=1, source_target_pairs={{0,128},{64,192},{128,0},{192,64},{1,129},{65,193},{129,1},{193,65... | collective-permute-start | bytes 393224 | tf_op jit(solution)/shard_map/ppermute | solution.py:134
  215.9 4.6 %collective-permute-start.21 = (bf16[128,512]{1,0:T(8,128)(2,1)S(1)}, bf16[128,512]{1,0:T(8,128)(2,1)S(1)}, u32[]{:S(2)}, u32[]{:S(2)}) collective-permute-start(bf16[128,512]{1,0:T(8,128)(2,1)S(1)} %add_convert_fusion.refs_5_), channel_id=1, source_target_pairs={{0,64},{64,128},{128,192},{1,65},{65,129},{129,193},{2,66},{66,130... | collective-permute-start | bytes 393224 | tf_op jit(solution)/shard_map/ppermute | solution.py:132
  223.8 3.6 %collective-permute-done.13.refs_4_ = bf16[128,512]{1,0:T(8,128)(2,1)S(1)} collective-permute-done((bf16[128,512]{1,0:T(8,128)(2,1)S(1)}, bf16[128,512]{1,0:T(8,128)(2,1)S(1)}, u32[]{:S(2)}, u32[]{:S(2)}) %collective-permute-start.13) | collective-permute-done | bytes 131104 | tf_op jit(solution)/shard_map/ppermute | solution.py:135
  (98 shorter events, 25.6 us)
Async XLA Ops:
  7.2 55.5 %all-gather.2.cloned.1.call-start = ((), (), s32[]{:S(2)}) async-start(), calls=%async_computation.4 | async-start | bytes 2359296 | tf_op jit(solution)/shard_map/all_gather | solution.py:491
  10.7 23.8 %copy-start = (bf16[512,1024]{1,0:T(8,128)(2,1)S(1)}, bf16[512,1024]{1,0:T(8,128)(2,1)}, u32[]{:S(2)}) copy-start(bf16[512,1024]{1,0:T(8,128)(2,1)} %table_ref.1) | copy-start | bytes 3145732
  15.4 28.1 %collective-permute-start = (bf16[256,1280]{1,0:T(8,128)(2,1)}, bf16[256,1280]{1,0:T(8,128)(2,1)}, u32[]{:S(2)}, u32[]{:S(2)}) collective-permute-start(bf16[256,1280]{1,0:T(8,128)(2,1)} %get-tuple-element.32.kv0_ref), channel_id=1, source_target_pairs={{0,64},{64,128},{128,192},{1,65},{65,129},{129,193},{2,66},{66,130... | collective-permute-start | bytes 1966088 | tf_op jit(solution)/shard_map/ppermute | solution.py:496
  21.3 12.8 %all-to-all-start = ((s32[32,1,48]{2,1,0:T(1,128)}), s32[32,1,48]{2,1,0:T(1,128)S(1)}, u32[]{:S(2)}, u32[]{:S(2)}) async-start(s32[32,1,48]{2,1,0:T(1,128)} %bitcast.7), calls=%async_computation | async-start | bytes 32768 | tf_op jit(solution)/shard_map/all_to_all | solution.py:506
  36.6 40.7 %all-to-all-start.1 = ((bf16[32,24,1024]{2,1,0:T(8,128)(2,1)}), bf16[32,24,1024]{2,1,0:T(8,128)(2,1)S(1)}, u32[]{:S(2)}, u32[]{:S(2)}) async-start(bf16[32,24,1024]{2,1,0:T(8,128)(2,1)} %bitcast.10), calls=%async_computation.1 | async-start | bytes 3145728 | tf_op jit(solution)/shard_map/all_to_all | solution.py:512
  43.7 24.5 %collective-permute-start.1 = (bf16[256,1280]{1,0:T(8,128)(2,1)}, bf16[256,1280]{1,0:T(8,128)(2,1)}, u32[]{:S(2)}, u32[]{:S(2)}) collective-permute-start(bf16[256,1280]{1,0:T(8,128)(2,1)} %collective-permute-done.kv1_ref), channel_id=1, source_target_pairs={{0,64},{64,128},{128,192},{1,65},{65,129},{129,193},{2,66},{66,130... | collective-permute-start | bytes 1966088 | tf_op jit(solution)/shard_map/ppermute | solution.py:496
  68.2 17.5 %collective-permute-start.2 = (bf16[256,1280]{1,0:T(8,128)(2,1)}, bf16[256,1280]{1,0:T(8,128)(2,1)}, u32[]{:S(2)}, u32[]{:S(2)}) collective-permute-start(bf16[256,1280]{1,0:T(8,128)(2,1)} %collective-permute-done.1.kv2_ref), channel_id=1, source_target_pairs={{0,64},{64,128},{128,192},{1,65},{65,129},{129,193},{2,66},{66,130... | collective-permute-start | bytes 1966088 | tf_op jit(solution)/shard_map/ppermute | solution.py:520
  77.3 28.6 %all-to-all-start.2 = ((bf16[32,24,1024]{2,1,0:T(8,128)(2,1)}), bf16[32,24,1024]{2,1,0:T(8,128)(2,1)}, u32[]{:S(2)}, u32[]{:S(2)}) async-start(bf16[32,24,1024]{2,1,0:T(8,128)(2,1)} %bitcast.12), calls=%async_computation.2 | async-start | bytes 3145728 | tf_op jit(solution)/shard_map/all_to_all | solution.py:517
  86.9 19.0 %copy-start.9 = (f32[1024,8]{0,1:T(8,128)S(1)}, f32[1024,8]{0,1:T(8,128)}, u32[]{:S(2)}) copy-start(f32[1024,8]{0,1:T(8,128)} %param.20) | copy-start | bytes 98308
  127.0 45.6 %all-to-all-start.3 = ((bf16[32,48,1024]{2,1,0:T(8,128)(2,1)}), bf16[32,48,1024]{2,1,0:T(8,128)(2,1)}, u32[]{:S(2)}, u32[]{:S(2)}) async-start(bf16[32,48,1024]{2,1,0:T(8,128)(2,1)} %bitcast.32), calls=%async_computation.3 | async-start | bytes 6291456 | tf_op jit(solution)/shard_map/all_to_all | solution.py:525
  177.9 6.4 %collective-permute-start.3 = (bf16[128,512]{1,0:T(8,128)(2,1)S(1)}, bf16[128,512]{1,0:T(8,128)(2,1)S(1)}, u32[]{:S(2)}, u32[]{:S(2)}) collective-permute-start(bf16[128,512]{1,0:T(8,128)(2,1)S(1)} %get-tuple-element.44), channel_id=1, source_target_pairs={{0,200},{64,0},{128,64},{192,128},{8,192},{72,8},{136,72},{200,136... | collective-permute-start | bytes 393224 | tf_op jit(solution)/shard_map/ppermute | solution.py:167
  179.8 6.9 %collective-permute-start.7 = (bf16[128,512]{1,0:T(8,128)(2,1)S(1)}, bf16[128,512]{1,0:T(8,128)(2,1)S(1)}, u32[]{:S(2)}, u32[]{:S(2)}) collective-permute-start(bf16[128,512]{1,0:T(8,128)(2,1)S(1)} %get-tuple-element.48), channel_id=1, source_target_pairs={{0,64},{64,128},{128,192},{192,8},{8,72},{72,136},{136,200},{200,0... | collective-permute-start | bytes 393224 | tf_op jit(solution)/shard_map/ppermute | solution.py:167
  180.0 7.1 %collective-permute-start.14 = (bf16[128,512]{1,0:T(8,128)(2,1)S(1)}, bf16[128,512]{1,0:T(8,128)(2,1)S(1)}, u32[]{:S(2)}, u32[]{:S(2)}) collective-permute-start(bf16[128,512]{1,0:T(8,128)(2,1)S(1)} %get-tuple-element.52), channel_id=1, source_target_pairs={{0,200},{64,0},{128,64},{192,128},{8,192},{72,8},{136,72},{200,136... | collective-permute-start | bytes 393224 | tf_op jit(solution)/shard_map/ppermute | solution.py:167
  183.0 7.1 %collective-permute-start.18 = (bf16[128,512]{1,0:T(8,128)(2,1)S(1)}, bf16[128,512]{1,0:T(8,128)(2,1)S(1)}, u32[]{:S(2)}, u32[]{:S(2)}) collective-permute-start(bf16[128,512]{1,0:T(8,128)(2,1)S(1)} %get-tuple-element.56), channel_id=1, source_target_pairs={{0,64},{64,128},{128,192},{192,8},{8,72},{72,136},{136,200},{200,0... | collective-permute-start | bytes 393224 | tf_op jit(solution)/shard_map/ppermute | solution.py:167
  184.4 6.2 %collective-permute-start.4 = (bf16[128,512]{1,0:T(8,128)(2,1)S(1)}, bf16[128,512]{1,0:T(8,128)(2,1)S(1)}, u32[]{:S(2)}, u32[]{:S(2)}) collective-permute-start(bf16[128,512]{1,0:T(8,128)(2,1)S(1)} %add_convert_fusion.11), channel_id=1, source_target_pairs={{0,200},{64,0},{128,64},{192,128},{8,192},{72,8},{136,72},{200,136... | collective-permute-start | bytes 393224 | tf_op jit(solution)/shard_map/ppermute | solution.py:167
  186.7 6.9 %collective-permute-start.8 = (bf16[128,512]{1,0:T(8,128)(2,1)S(1)}, bf16[128,512]{1,0:T(8,128)(2,1)S(1)}, u32[]{:S(2)}, u32[]{:S(2)}) collective-permute-start(bf16[128,512]{1,0:T(8,128)(2,1)S(1)} %add_convert_fusion.8), channel_id=1, source_target_pairs={{0,64},{64,128},{128,192},{192,8},{8,72},{72,136},{136,200},{200,0... | collective-permute-start | bytes 393224 | tf_op jit(solution)/shard_map/ppermute | solution.py:167
  187.1 6.6 %collective-permute-start.15 = (bf16[128,512]{1,0:T(8,128)(2,1)S(1)}, bf16[128,512]{1,0:T(8,128)(2,1)S(1)}, u32[]{:S(2)}, u32[]{:S(2)}) collective-permute-start(bf16[128,512]{1,0:T(8,128)(2,1)S(1)} %add_convert_fusion.5), channel_id=1, source_target_pairs={{0,200},{64,0},{128,64},{192,128},{8,192},{72,8},{136,72},{200,136... | collective-permute-start | bytes 393224 | tf_op jit(solution)/shard_map/ppermute | solution.py:167
  190.2 7.4 %collective-permute-start.19 = (bf16[128,512]{1,0:T(8,128)(2,1)S(1)}, bf16[128,512]{1,0:T(8,128)(2,1)S(1)}, u32[]{:S(2)}, u32[]{:S(2)}) collective-permute-start(bf16[128,512]{1,0:T(8,128)(2,1)S(1)} %add_convert_fusion.2), channel_id=1, source_target_pairs={{0,64},{64,128},{128,192},{192,8},{8,72},{72,136},{136,200},{200,0... | collective-permute-start | bytes 393224 | tf_op jit(solution)/shard_map/ppermute | solution.py:167
  190.5 7.1 %collective-permute-start.5 = (bf16[128,512]{1,0:T(8,128)(2,1)S(1)}, bf16[128,512]{1,0:T(8,128)(2,1)S(1)}, u32[]{:S(2)}, u32[]{:S(2)}) collective-permute-start(bf16[128,512]{1,0:T(8,128)(2,1)S(1)} %add_convert_fusion.10), channel_id=1, source_target_pairs={{0,200},{64,0},{128,64},{192,128},{8,192},{72,8},{136,72},{200,136... | collective-permute-start | bytes 393224 | tf_op jit(solution)/shard_map/ppermute | solution.py:167
  193.6 10.7 %collective-permute-start.9 = (bf16[128,512]{1,0:T(8,128)(2,1)S(1)}, bf16[128,512]{1,0:T(8,128)(2,1)S(1)}, u32[]{:S(2)}, u32[]{:S(2)}) collective-permute-start(bf16[128,512]{1,0:T(8,128)(2,1)S(1)} %add_convert_fusion.7), channel_id=1, source_target_pairs={{0,64},{64,128},{128,192},{192,8},{8,72},{72,136},{136,200},{200,0... | collective-permute-start | bytes 393224 | tf_op jit(solution)/shard_map/ppermute | solution.py:167
  193.8 7.5 %collective-permute-start.16 = (bf16[128,512]{1,0:T(8,128)(2,1)S(1)}, bf16[128,512]{1,0:T(8,128)(2,1)S(1)}, u32[]{:S(2)}, u32[]{:S(2)}) collective-permute-start(bf16[128,512]{1,0:T(8,128)(2,1)S(1)} %add_convert_fusion.4), channel_id=1, source_target_pairs={{0,200},{64,0},{128,64},{192,128},{8,192},{72,8},{136,72},{200,136... | collective-permute-start | bytes 393224 | tf_op jit(solution)/shard_map/ppermute | solution.py:167
  197.6 10.5 %collective-permute-start.20 = (bf16[128,512]{1,0:T(8,128)(2,1)S(1)}, bf16[128,512]{1,0:T(8,128)(2,1)S(1)}, u32[]{:S(2)}, u32[]{:S(2)}) collective-permute-start(bf16[128,512]{1,0:T(8,128)(2,1)S(1)} %add_convert_fusion.1), channel_id=1, source_target_pairs={{0,64},{64,128},{128,192},{192,8},{8,72},{72,136},{136,200},{200,0... | collective-permute-start | bytes 393224 | tf_op jit(solution)/shard_map/ppermute | solution.py:167
  197.7 6.6 %collective-permute-start.6 = (bf16[128,512]{1,0:T(8,128)(2,1)S(1)}, bf16[128,512]{1,0:T(8,128)(2,1)S(1)}, u32[]{:S(2)}, u32[]{:S(2)}) collective-permute-start(bf16[128,512]{1,0:T(8,128)(2,1)S(1)} %add_convert_fusion.9), channel_id=1, source_target_pairs={{0,200},{64,0},{128,64},{192,128},{8,192},{72,8},{136,72},{200,136... | collective-permute-start | bytes 393224 | tf_op jit(solution)/shard_map/ppermute | solution.py:167
  201.3 6.7 %collective-permute-start.17 = (bf16[128,512]{1,0:T(8,128)(2,1)S(1)}, bf16[128,512]{1,0:T(8,128)(2,1)S(1)}, u32[]{:S(2)}, u32[]{:S(2)}) collective-permute-start(bf16[128,512]{1,0:T(8,128)(2,1)S(1)} %add_convert_fusion.3), channel_id=1, source_target_pairs={{0,200},{64,0},{128,64},{192,128},{8,192},{72,8},{136,72},{200,136... | collective-permute-start | bytes 393224 | tf_op jit(solution)/shard_map/ppermute | solution.py:167
  204.4 11.5 %collective-permute-start.12 = (bf16[128,512]{1,0:T(8,128)(2,1)S(1)}, bf16[128,512]{1,0:T(8,128)(2,1)S(1)}, u32[]{:S(2)}, u32[]{:S(2)}) collective-permute-start(bf16[128,512]{1,0:T(8,128)(2,1)S(1)} %add_convert_fusion.6.refs_0_), channel_id=1, source_target_pairs={{0,128},{64,192},{128,0},{192,64},{1,129},{65,193},{129,1},{193,65... | collective-permute-start | bytes 393224 | tf_op jit(solution)/shard_map/ppermute | solution.py:134
  206.7 13.7 %collective-permute-start.11 = (bf16[128,512]{1,0:T(8,128)(2,1)S(1)}, bf16[128,512]{1,0:T(8,128)(2,1)S(1)}, u32[]{:S(2)}, u32[]{:S(2)}) collective-permute-start(bf16[128,512]{1,0:T(8,128)(2,1)S(1)} %add_convert_fusion.6.refs_0_), channel_id=1, source_target_pairs={{64,0},{128,64},{192,128},{65,1},{129,65},{193,129},{66,2},{130,66... | collective-permute-start | bytes 393224 | tf_op jit(solution)/shard_map/ppermute | solution.py:133
  208.1 13.7 %collective-permute-start.23 = (bf16[128,512]{1,0:T(8,128)(2,1)S(1)}, bf16[128,512]{1,0:T(8,128)(2,1)S(1)}, u32[]{:S(2)}, u32[]{:S(2)}) collective-permute-start(bf16[128,512]{1,0:T(8,128)(2,1)S(1)} %add_convert_fusion.refs_5_), channel_id=1, source_target_pairs={{0,128},{64,192},{128,0},{192,64},{1,129},{65,193},{129,1},{193,65... | collective-permute-start | bytes 393224 | tf_op jit(solution)/shard_map/ppermute | solution.py:134
  213.2 10.5 %collective-permute-start.10 = (bf16[128,512]{1,0:T(8,128)(2,1)S(1)}, bf16[128,512]{1,0:T(8,128)(2,1)S(1)}, u32[]{:S(2)}, u32[]{:S(2)}) collective-permute-start(bf16[128,512]{1,0:T(8,128)(2,1)S(1)} %add_convert_fusion.6.refs_0_), channel_id=1, source_target_pairs={{0,64},{64,128},{128,192},{1,65},{65,129},{129,193},{2,66},{66,130... | collective-permute-start | bytes 393224 | tf_op jit(solution)/shard_map/ppermute | solution.py:132
  214.6 9.2 %collective-permute-start.22 = (bf16[128,512]{1,0:T(8,128)(2,1)S(1)}, bf16[128,512]{1,0:T(8,128)(2,1)S(1)}, u32[]{:S(2)}, u32[]{:S(2)}) collective-permute-start(bf16[128,512]{1,0:T(8,128)(2,1)S(1)} %add_convert_fusion.refs_5_), channel_id=1, source_target_pairs={{64,0},{128,64},{192,128},{65,1},{129,65},{193,129},{66,2},{130,66... | collective-permute-start | bytes 393224 | tf_op jit(solution)/shard_map/ppermute | solution.py:133
  215.9 7.9 %collective-permute-start.21 = (bf16[128,512]{1,0:T(8,128)(2,1)S(1)}, bf16[128,512]{1,0:T(8,128)(2,1)S(1)}, u32[]{:S(2)}, u32[]{:S(2)}) collective-permute-start(bf16[128,512]{1,0:T(8,128)(2,1)S(1)} %add_convert_fusion.refs_5_), channel_id=1, source_target_pairs={{0,64},{64,128},{128,192},{1,65},{65,129},{129,193},{2,66},{66,130... | collective-permute-start | bytes 393224 | tf_op jit(solution)/shard_map/ppermute | solution.py:132
  220.5 6.9 %collective-permute-start.13 = (bf16[128,512]{1,0:T(8,128)(2,1)S(1)}, bf16[128,512]{1,0:T(8,128)(2,1)S(1)}, u32[]{:S(2)}, u32[]{:S(2)}) collective-permute-start(bf16[128,512]{1,0:T(8,128)(2,1)S(1)} %collective-permute-done.12.refs_3_), channel_id=1, source_target_pairs={{128,192},{64,0},{129,193},{65,1},{130,194},{66,2},{131,195},{67,3... | collective-permute-start | bytes 393224 | tf_op jit(solution)/shard_map/ppermute | solution.py:135
  221.8 7.0 %collective-permute-start.24 = (bf16[128,512]{1,0:T(8,128)(2,1)S(1)}, bf16[128,512]{1,0:T(8,128)(2,1)S(1)}, u32[]{:S(2)}, u32[]{:S(2)}) collective-permute-start(bf16[128,512]{1,0:T(8,128)(2,1)S(1)} %collective-permute-done.23.refs_8_), channel_id=1, source_target_pairs={{128,192},{64,0},{129,193},{65,1},{130,194},{66,2},{131,195},{67,3... | collective-permute-start | bytes 393224 | tf_op jit(solution)/shard_map/ppermute | solution.py:135
  (14 other events, 89.3 us)
Sparse Core Ops, SparseCore 0:
  10.4 52.2 all-gather.1
